TPU v7x, 128 devices: a whole 4x4x4 slice. The times are simulated.
128 devices in a mesh: seq: 16 (over x, y), dp: 8 (over z, core).
Axes of the slice: x: 4, y: 4, z: 4, core: 2. Of those that a mesh axis runs over, the one named last changes fastest.
Arguments:
- layer_input: bfloat16 [8, 5120, 6144], P('dp', 'seq'), may hold values from -6 to 6
- queries: bfloat16 [8, 5120, 4096], P('dp', 'seq'), may hold values from -6 to 6
- key_vectors: bfloat16 [8, 5120, 4096], P('dp', 'seq'), may hold values from -6 to 6
- value_vectors: bfloat16 [8, 5120, 4096], P('dp', 'seq'), may hold values from -6 to 6
- grad_attended: bfloat16 [8, 5120, 4096], P('dp', 'seq'), may hold values from -6 to 6
- log_decay: float32 [8, 32, 5120], P('dp', None, 'seq'), may hold values from -2 to 0, as said below
- kept_blocks: int32 [128], replicated, may hold values from 0 to 4607, as said below
Outputs:
- attended: bfloat16 [8, 5120, 4096], P('dp', 'seq')
- grad_queries: bfloat16 [8, 5120, 4096], P('dp', 'seq')
- grad_keys: bfloat16 [8, 5120, 4096], P('dp', 'seq')
- grad_values: bfloat16 [8, 5120, 4096], P('dp', 'seq')
- grad_blocks: float32 [128, 128, 128], P(('seq', 'dp'))
Inputs may be any that keep to these rules, and one draw needn't show every extreme that they name: `kept_blocks`: distinct block numbers of the 48 x 96 blocks, row block major. `log_decay`: negative.
All inputs are finite; a program needn't handle non-finite values.
Results may differ from a plain program's by a relative error of at most 0.025.
Values may be sent and summed in bfloat16 or wider, within the bound.
No kernel may reach another device: no remote copies, remote signals or barrier semaphores. Data moves between devices by JAX's collectives and lax.ppermute only.
A program may use at most 192 MiB of HBM per device.

v0:
```python
import math

import jax
import jax.numpy as jnp
from jax import lax
from jax.sharding import PartitionSpec as P

BLOCK = 128


def per_device(
    layer_input, queries, key_vectors, value_vectors, grad_attended, log_decay, kept_blocks
):
    head_count = log_decay.shape[1]
    length = queries.shape[1]
    inner_width = queries.shape[2]
    head_dim = inner_width // head_count
    query_rows = queries[0].reshape(length, head_count, head_dim)
    key_rows = key_vectors[0].reshape(length, head_count, head_dim)
    value_rows = value_vectors[0].reshape(length, head_count, head_dim)
    upstream = grad_attended[0].reshape(length, head_count, head_dim).astype(jnp.float32)
    cumulative = jnp.cumsum(log_decay[0], axis=1)
    block_log = cumulative[:, -1]
    causal = jnp.tril(jnp.ones((length, length), dtype=bool))
    log_gaps = cumulative[:, :, None] - cumulative[:, None, :]
    within = jnp.where(causal, jnp.exp(jnp.minimum(log_gaps, 0.0)), 0.0)
    scores = jnp.einsum("thc,shc->hts", query_rows, key_rows, preferred_element_type=jnp.float32)
    weights = (scores * within).astype(jnp.bfloat16)
    tail_decay = jnp.exp(block_log[:, None] - cumulative).T[:, :, None]
    head_decay = jnp.exp(cumulative).T[:, :, None]
    scaled_keys = (tail_decay * key_rows).astype(jnp.bfloat16)
    scaled_queries = (head_decay * query_rows).astype(jnp.bfloat16)
    block_state = jnp.einsum(
        "shc,she->hce", scaled_keys, value_rows, preferred_element_type=jnp.float32
    ).astype(jnp.bfloat16)
    block_index = lax.axis_index("seq")
    all_logs = lax.all_gather(block_log[None, :], "seq", axis=0, tiled=True)
    inclusive = jnp.cumsum(all_logs, axis=0)
    own_inclusive = lax.dynamic_index_in_dim(inclusive, block_index, 0, keepdims=False)
    own_exclusive = own_inclusive - block_log
    gathered = lax.all_gather(block_state[None], "seq", axis=0, tiled=True)
    sources = jnp.arange(gathered.shape[0])
    source_incl = inclusive
    factor = jnp.where(
        (sources < block_index)[:, None],
        jnp.exp(jnp.minimum(own_exclusive[None, :] - source_incl, 0.0)),
        0.0,
    )
    carried = jnp.einsum("nh,nhce->hce", factor, gathered.astype(jnp.float32))
    carried = carried.astype(jnp.bfloat16)
    raw_output = jnp.einsum("hts,she->the", weights, value_rows, preferred_element_type=jnp.float32)
    raw_output = raw_output + jnp.einsum(
        "thc,hce->the", scaled_queries, carried, preferred_element_type=jnp.float32
    )
    inverse = lax.rsqrt(jnp.mean(raw_output * raw_output, axis=2, keepdims=True) + 1e-06)
    normed = raw_output * inverse
    grad_raw = (
        inverse * (upstream - normed * jnp.mean(upstream * normed, axis=2, keepdims=True))
    ).astype(jnp.bfloat16)
    block_grad = jnp.einsum(
        "thc,the->hce", scaled_queries, grad_raw, preferred_element_type=jnp.float32
    ).astype(jnp.bfloat16)
    gathered = lax.all_gather(block_grad[None], "seq", axis=0, tiled=True)
    sources = jnp.arange(gathered.shape[0])
    source_incl = inclusive
    source_excl = source_incl - all_logs
    factor = jnp.where(
        (sources > block_index)[:, None],
        jnp.exp(jnp.minimum(source_excl - own_inclusive[None, :], 0.0)),
        0.0,
    )
    later_grad = jnp.einsum("nh,nhce->hce", factor, gathered.astype(jnp.float32))
    later_grad = later_grad.astype(jnp.bfloat16)
    dscores = (
        jnp.einsum("the,she->hts", grad_raw, value_rows, preferred_element_type=jnp.float32)
        * within
    ).astype(jnp.bfloat16)
    grad_q = jnp.einsum("hts,shc->thc", dscores, key_rows, preferred_element_type=jnp.float32)
    grad_q = grad_q + head_decay * jnp.einsum(
        "the,hce->thc", grad_raw, carried, preferred_element_type=jnp.float32
    )
    grad_k = jnp.einsum("hts,thc->shc", dscores, query_rows, preferred_element_type=jnp.float32)
    grad_k = grad_k + tail_decay * jnp.einsum(
        "she,hce->shc", value_rows, later_grad, preferred_element_type=jnp.float32
    )
    grad_v = jnp.einsum("hts,the->she", weights, grad_raw, preferred_element_type=jnp.float32)
    grad_v = grad_v + jnp.einsum(
        "shc,hce->she", scaled_keys, later_grad, preferred_element_type=jnp.float32
    )
    grad_q = grad_q.astype(jnp.bfloat16).reshape(length, inner_width)
    grad_k = grad_k.astype(jnp.bfloat16).reshape(length, inner_width)
    grad_v = grad_v.astype(jnp.bfloat16).reshape(length, inner_width)
    stacked = jnp.concatenate([grad_q, grad_k, grad_v], axis=1)
    col_blocks = stacked.reshape(length, -1, BLOCK)
    row_blocks = layer_input[0].reshape(length, -1, BLOCK)
    per_row = col_blocks.shape[1]
    devices_all = lax.axis_size("seq") * lax.axis_size("dp")
    token_scale = 1.0 / math.sqrt(length * devices_all)
    input_cols = jnp.take(row_blocks, kept_blocks // per_row, axis=1)
    grad_cols = jnp.take(col_blocks, kept_blocks % per_row, axis=1)
    grad_blocks = lax.psum_scatter(
        jnp.einsum("tkr,tkc->krc", input_cols, grad_cols, preferred_element_type=jnp.float32)
        * token_scale,
        ("seq", "dp"),
        scatter_dimension=0,
        tiled=True,
    )
    attended = normed.astype(jnp.bfloat16).reshape(1, length, inner_width)
    return (
        attended,
        grad_q.reshape(1, length, inner_width),
        grad_k.reshape(1, length, inner_width),
        grad_v.reshape(1, length, inner_width),
        grad_blocks,
    )


def solution(mesh):
    placed = (
        P("dp", "seq", None),
        P("dp", "seq", None),
        P("dp", "seq", None),
        P("dp", "seq", None),
        P("dp", "seq", None),
        P("dp", None, "seq"),
        P(),
    )
    return jax.shard_map(
        per_device,
        mesh=mesh,
        in_specs=placed,
        out_specs=(
            P("dp", "seq", None),
            P("dp", "seq", None),
            P("dp", "seq", None),
            P("dp", "seq", None),
            P(("seq", "dp"), None, None),
        ),
        check_vma=False,
    )
```

profile of v0, /device:TPU:0, one launch (start us, length us, event | category | flops | bytes accessed | tf_op | source)
XLA Modules:
  0.0 1008.2 jit_solution(11887763262611355788)
XLA Ops:
  7.2 0.0 all-gather.6.cloned.1.call-start
  7.2 0.8 copy_bitcast_fusion.1
  8.0 0.9 reduce-window.6
  8.9 0.2 slice_reduce_fusion
  9.1 0.1 copy_bitcast_fusion
  9.2 0.2 slice_reduce_fusion.1
  9.4 0.1 exponential_bitcast_fusion.1
  9.5 2.5 copy.96
  12.0 0.6 copy.97
  12.7 0.0 copy-start.20
  12.7 0.8 copy-done.7
  13.5 8.6 fusion.40
  22.1 0.0 all-gather.6.cloned.1.call-update
  22.1 0.0 all-gather.8.cloned.1.call-start
  22.2 0.6 dynamic-slice
  23.5 0.2 dynamic-update-slice
  23.7 41.1 %all-reduce.1 = f32[512]{0:T(512)S(1)} all-reduce(f32[512]{0:T(512)S(1)} %dynamic-update-slice), channel_id=2, replica_groups=mesh['seq'=16,'dp'=8] {'seq'}, use_global_device_ids=true, to_apply=%add.1 | all-reduce | flops 512 | bytes 4096
  64.8 0.1 reshape.90
  65.0 0.1 select_bitcast_fusion
  65.1 0.1 copy.85
  65.2 3.3 copy.95
  68.5 0.3 copy-done.18
  68.8 0.6 convert_bitcast_fusion
  69.4 3.3 copy.98
  72.8 8.2 multiply_convert_fusion.1
  81.0 3.1 copy-done
  84.1 5.8 fusion.27
  89.9 46.4 %all-gather.6.cloned.1.call-done = bf16[512,128,128]{2,1,0:T(8,128)(2,1)} async-done(((bf16[32,128,128]{2,1,0:T(8,128)(2,1)}), bf16[512,128,128]{2,1,0:T(8,128)(2,1)}) %all-gather.6.cloned.1.call-update) | async-done | bytes 16777232 | tf_op jit(solution)/shard_map/all_gather | solution.py:41
  136.3 15.7 %fusion.2 = f32[32,1,128,128]{3,1,2,0:T(1,128)S(1)} fusion(bf16[16,32,1,1]{0,2,3,1:T(2,128)(2,1)S(1)} %copy.85, bf16[16,32,128,128]{3,2,1,0:T(8,128)(2,1)} %bitcast.93), kind=kOutput, calls=%fused_computation.4 | convolution fusion | flops 16777216 | bytes 18875392 | tf_op jit(solution)/shard_map/nh,nhce->hce/dot_general | solution.py:49
  152.0 6.0 multiply_reduce_fusion.1
  158.1 6.4 multiply_reduce_fusion
  164.5 0.0 copy-start.15
  164.5 7.9 multiply_convert_fusion.2
  172.4 1.5 copy-done.3
  173.8 6.0 fusion.39
  179.9 0.0 all-gather.8.cloned.1.call-update
  179.9 0.0 reduce-scatter.2.cloned.1.call-start
  180.0 0.1 copy.89
  180.1 3.0 copy.99
  183.1 2.9 copy.84
  186.1 10.0 gather_fusion
  196.1 9.9 multiply_convert_fusion
  206.0 3.3 fusion.30
  209.3 3.5 fusion.14
  212.8 8.6 fusion.35
  221.4 69.6 %all-gather.8.cloned.1.call-done = bf16[512,128,128]{2,1,0:T(8,128)(2,1)} async-done(((bf16[32,128,128]{2,1,0:T(8,128)(2,1)}), bf16[512,128,128]{2,1,0:T(8,128)(2,1)}) %all-gather.8.cloned.1.call-update) | async-done | bytes 16777232 | tf_op jit(solution)/shard_map/all_gather | solution.py:63
  291.0 15.8 %fusion = f32[32,1,128,128]{3,1,2,0:T(1,128)S(1)} fusion(bf16[16,32,1,1]{0,2,3,1:T(2,128)(2,1)S(1)} %copy.89, bf16[16,32,128,128]{3,2,1,0:T(8,128)(2,1)} %bitcast.94), kind=kOutput, calls=%fused_computation.2 | convolution fusion | flops 16777216 | bytes 18875392 | tf_op jit(solution)/shard_map/nh,nhce->hce/dot_general | solution.py:72
  306.8 4.8 fusion.17
  311.7 7.3 fusion.16
  319.0 5.3 fusion.12
  324.4 4.0 pad_maximum_fusion
  328.4 10.9 %gather_fusion.1 = bf16[128,320,128]{2,1,0:T(8,128)(2,1)} fusion(bf16[320,96,128]{2,0,1:T(8,128)(2,1)} %pad_maximum_fusion, s32[1024]{0:T(1024)S(1)} %get-tuple-element.24), kind=kCustom, calls=%fused_computation.1 | custom fusion | bytes 20972032 | tf_op jit(solution)/shard_map/jit(_take)/gather | solution.py:100
  339.3 11.8 %broadcast_multiply_fusion = f32[128,128,128]{2,1,0:T(8,128)} fusion(bf16[128,320,128]{2,1,0:T(8,128)(2,1)} %gather_fusion.1, pred[128]{0:T(512)(128)(4,1)S(1)} %get-tuple-element.18, bf16[128,320,128]{2,1,0:T(8,128)(2,1)} %gather_fusion, pred[128]{0:T(512)(128)(4,1)S(1)} %get-tuple-element.5), kind=kOutput, calls=%fused_computation.33 | convolution fusion | flops 1354760192 | bytes 29360384 | tf_op jit(solution)/shard_map/tkr,tkc->krc/dot_general | solution.py:102
  351.1 0.0 reduce-scatter.2.cloned.1.call-update
  351.1 1.7 copy-done.11
  352.8 3.2 copy.77
  356.0 5.2 reshape_reshape.9
  361.2 5.1 copy.72
  366.2 5.2 reshape.72
  371.4 3.2 copy.83
  374.6 3.2 copy.81
  377.8 3.1 reshape_reshape.11
  380.9 5.2 reshape_reshape.10
  386.1 615.4 %reduce-scatter.2.cloned.1.call-done = f32[1,128,128]{2,1,0:T(8,128)} async-done(((f32[128,128,128]{2,1,0:T(8,128)}), f32[1,128,128]{2,1,0:T(8,128)}) %reduce-scatter.2.cloned.1.call-update) | async-done | bytes 65552 | tf_op jit(solution)/shard_map/reduce_scatter | solution.py:101
  (45 shorter events, 0.3 us)
Async XLA Ops:
  7.2 129.2 %all-gather.6.cloned.1.call-start = ((), (), s32[]{:S(2)}) async-start(), calls=%async_computation.2 | async-start | bytes 17825792 | tf_op jit(solution)/shard_map/all_gather | solution.py:41
  9.1 2.9 copy-start.17
  12.0 1.5 copy-start.7
  12.6 68.4 %copy-start.6 = (bf16[40,8,32,128]{3,2,1,0:T(8,128)(2,1)}, bf16[40,8,32,128]{3,2,1,0:T(8,128)(2,1)S(1)}, u32[]{:S(2)}) copy-start(bf16[40,8,32,128]{3,2,1,0:T(8,128)(2,1)S(1)} %copy.97) | copy-start | bytes 7864324
  12.7 9.5 copy-start.20
  22.1 268.8 %all-gather.8.cloned.1.call-start = ((), (), s32[]{:S(2)}) async-start(), calls=%async_computation.3 | async-start | bytes 17825792 | tf_op jit(solution)/shard_map/all_gather | solution.py:63
  65.2 3.6 copy-start.18
  68.8 4.0 copy-start.14
  69.4 3.4 copy-start.8
  81.0 3.1 copy-start
  164.5 9.4 copy-start.15
  172.4 1.5 copy-start.3
  179.9 821.5 %reduce-scatter.2.cloned.1.call-start = ((), (), s32[]{:S(2)}) async-start(), calls=%async_computation.1 | async-start | bytes 8454144 | tf_op jit(solution)/shard_map/reduce_scatter | solution.py:101
  183.1 2.9 copy-start.19
  196.1 10.0 copy-start.9
  206.0 3.3 copy-start.4
  306.8 4.8 copy-start.5
  319.0 5.3 copy-start.1
  319.0 5.3 copy-start.10
  324.4 4.0 copy-start.12
  351.1 1.7 copy-start.11
  361.2 10.3 %copy-start.2 = (bf16[320,32,128]{2,0,1:T(8,128)(2,1)S(1)}, bf16[320,32,128]{2,0,1:T(8,128)(2,1)}, u32[]{:S(2)}) copy-start(bf16[320,32,128]{2,0,1:T(8,128)(2,1)} %copy-done.1) | copy-start | bytes 7864324
  371.4 3.2 copy-start.13
  374.6 3.2 copy-start.16
Sparse Core Ops, SparseCore 0:
  22.3 114.0 all-gather.5
  180.0 110.8 all-gather.7
  351.2 650.1 reduce-scatter.1
where the time goes:
time: 1020 us; the launch traced here: 1010 us
  waiting for transfers between devices  731 us (72%)
  matrix products  121 us (12%)
  local copies, waits for them, and re-layouts  79.6 us (8%)
  blocking collectives  41.1 us (4%)
  other arithmetic  20.2 us (2%)
  between operations  15 us (1%)
    reduce_scatter x1, waiting for transfers between devices, per_device(): lax.psum_scatter(jnp.einsum('tkr,tkc->krc', input_cols, grad_cols, prefer...  615 us
    all_gather x1, waiting for transfers between devices, per_device(): gathered = lax.all_gather(block_grad[None], 'seq', axis=0, tiled=True)  69.6 us
    all_gather x1, waiting for transfers between devices, per_device(): gathered = lax.all_gather(block_state[None], 'seq', axis=0, tiled=True)  46.4 us
    unnamed x1, blocking collectives  41.1 us
    unnamed x50, local copies, waits for them, and re-layouts  21.1 us
  transfers between devices with their start and end apart: 3, of which 3 were waited for; matrix products, arithmetic and copies ran while one was open for 10% of the time, Pallas kernels for 0%

commit v1 on v0

v1 whole, which is shorter than its diff:
```python
import functools
import math

import jax
import jax.numpy as jnp
from jax import lax
from jax.experimental import pallas as pl
from jax.experimental.pallas import tpu as pltpu
from jax.sharding import Mesh
from jax.sharding import PartitionSpec as P

BLOCK = 128
GROUP = 8
AUX = 16
F32 = jnp.float32
BF16 = jnp.bfloat16
MIB = 1 << 20


def dot_nt(a, b):
    return lax.dot_general(a, b, (((1,), (1,)), ((), ())), preferred_element_type=F32)


def dot_nn(a, b):
    return lax.dot_general(a, b, (((1,), (0,)), ((), ())), preferred_element_type=F32)


def dot_tn(a, b):
    return lax.dot_general(a, b, (((0,), (0,)), ((), ())), preferred_element_type=F32)


def head_slice(h):
    return slice(h * BLOCK, (h + 1) * BLOCK)


def row_cuts(length):
    return [(r, min(r + BLOCK, length)) for r in range(0, length, BLOCK)]


def states_kernel(decay_ref, k_ref, v_ref, payload_ref, col_ref, row_ref):
    length = k_ref.shape[1]
    decay = decay_ref[0]
    high = decay.astype(BF16).astype(F32)
    rest = decay - high
    middle = rest.astype(BF16).astype(F32)
    terms = jnp.concatenate([high, middle, rest - middle], axis=0).astype(BF16)
    t = lax.broadcasted_iota(jnp.int32, (length, length), 0)
    s = lax.broadcasted_iota(jnp.int32, (length, length), 1)
    lower = jnp.where(s <= t, 1.0, 0.0).astype(BF16)
    upper = jnp.where(t <= s, 1.0, 0.0).astype(BF16)
    cols = dot_nt(lower, terms)
    col = cols[:, :GROUP] + cols[:, GROUP : 2 * GROUP] + cols[:, 2 * GROUP :]
    rows = dot_nn(terms, upper)
    row = rows[:GROUP] + rows[GROUP : 2 * GROUP] + rows[2 * GROUP :]
    col_ref[0] = col
    row_ref[0] = row
    total = col[length - 1 : length, :]
    tail = jnp.exp(total - col)
    whole = jnp.exp(total)
    index = lax.broadcasted_iota(jnp.int32, (AUX, BLOCK), 0)
    for h in range(GROUP):
        keys = k_ref[0, :, head_slice(h)].astype(F32)
        scaled = (keys * tail[:, h : h + 1]).astype(BF16)
        state = dot_tn(scaled, v_ref[0, :, head_slice(h)])
        payload_ref[h // 2, head_slice(h % 2), :] = state.astype(BF16)
    for p in range(GROUP // 2):
        aux = jnp.zeros((AUX, BLOCK), F32)
        for i in range(2):
            value = jnp.broadcast_to(whole[:, 2 * p + i : 2 * p + i + 1], (AUX, BLOCK))
            first = value.astype(BF16).astype(F32)
            aux = jnp.where(index == 2 * i, first, aux)
            aux = jnp.where(index == 2 * i + 1, value - first, aux)
        payload_ref[p, 2 * BLOCK :, :] = aux.astype(BF16)


def scan_kernel(reverse, x_ref, aux_ref, out_ref):
    blocks = x_ref.shape[0]
    running = [jnp.zeros((BLOCK, BLOCK), F32) for _ in range(2)]
    for step in range(blocks):
        j = blocks - 1 - step if reverse else step
        aux = aux_ref[j].astype(F32)
        for i in range(2):
            out_ref[j, head_slice(i), :] = running[i].astype(BF16)
            whole = aux[2 * i : 2 * i + 1] + aux[2 * i + 1 : 2 * i + 2]
            running[i] = running[i] * whole + x_ref[j, head_slice(i), :].astype(F32)


def intra_kernel(q_ref, k_ref, v_ref, col_ref, row_ref, raw_ref):
    length = q_ref.shape[1]
    col = col_ref[0]
    for h in range(GROUP):
        sl = head_slice(h)
        for r0, r1 in row_cuts(length):
            scores = dot_nt(q_ref[0, r0:r1, sl], k_ref[0, :r1, sl])
            within = jnp.exp(col[r0:r1, h : h + 1] - row_ref[0, h : h + 1, :r1])
            t = lax.broadcasted_iota(jnp.int32, (r1 - r0, r1), 0) + r0
            s = lax.broadcasted_iota(jnp.int32, (r1 - r0, r1), 1)
            weights = (scores * jnp.where(s <= t, within, 0.0)).astype(BF16)
            raw_ref[0, r0:r1, sl] = dot_nn(weights, v_ref[0, :r1, sl])


def norm_kernel(raw_ref, q_ref, g_ref, col_ref, carried_ref, attended_ref, grad_raw_ref, grad_ref):
    head_decay = jnp.exp(col_ref[0])
    for h in range(GROUP):
        sl = head_slice(h)
        scaled = (q_ref[0, :, sl].astype(F32) * head_decay[:, h : h + 1]).astype(BF16)
        raw = raw_ref[0, :, sl] + dot_nn(scaled, carried_ref[h])
        inverse = lax.rsqrt(jnp.mean(raw * raw, axis=1, keepdims=True) + 1e-6)
        normed = raw * inverse
        upstream = g_ref[0, :, sl].astype(F32)
        shared = jnp.mean(upstream * normed, axis=1, keepdims=True)
        grad_raw = (inverse * (upstream - normed * shared)).astype(BF16)
        attended_ref[0, :, sl] = normed.astype(BF16)
        grad_raw_ref[0, :, sl] = grad_raw
        grad_ref[h] = dot_tn(scaled, grad_raw).astype(BF16)


def grad_q_kernel(
    grad_raw_ref, k_ref, v_ref, col_ref, row_ref, carried_ref, grad_q_ref, by_head_ref
):
    length = k_ref.shape[1]
    col = col_ref[0]
    head_decay = jnp.exp(col)
    for h in range(GROUP):
        sl = head_slice(h)
        for r0, r1 in row_cuts(length):
            grad_raw = grad_raw_ref[0, r0:r1, sl]
            scores = dot_nt(grad_raw, v_ref[0, :r1, sl])
            within = jnp.exp(col[r0:r1, h : h + 1] - row_ref[0, h : h + 1, :r1])
            t = lax.broadcasted_iota(jnp.int32, (r1 - r0, r1), 0) + r0
            s = lax.broadcasted_iota(jnp.int32, (r1 - r0, r1), 1)
            dscores = (scores * jnp.where(s <= t, within, 0.0)).astype(BF16)
            grad_q = dot_nn(dscores, k_ref[0, :r1, sl])
            grad_q = grad_q + head_decay[r0:r1, h : h + 1] * dot_nt(grad_raw, carried_ref[h])
            grad_q = grad_q.astype(BF16)
            grad_q_ref[0, r0:r1, sl] = grad_q
            by_head_ref[h, r0:r1, :] = grad_q


def grad_kv_kernel(
    grad_raw_ref, q_ref, k_ref, v_ref, col_ref, row_ref, grad_k_ref, grad_v_ref
):
    length = k_ref.shape[1]
    col = col_ref[0]
    for h in range(GROUP):
        sl = head_slice(h)
        for s0, s1 in row_cuts(length):
            queries = q_ref[0, s0:, sl]
            grad_raw = grad_raw_ref[0, s0:, sl]
            within = jnp.exp(row_ref[0, h : h + 1, s0:] - col[s0:s1, h : h + 1])
            s = lax.broadcasted_iota(jnp.int32, (s1 - s0, length - s0), 0)
            t = lax.broadcasted_iota(jnp.int32, (s1 - s0, length - s0), 1)
            within = jnp.where(s <= t, within, 0.0)
            weights = (dot_nt(k_ref[0, s0:s1, sl], queries) * within).astype(BF16)
            dscores = (dot_nt(v_ref[0, s0:s1, sl], grad_raw) * within).astype(BF16)
            grad_k_ref[0, s0:s1, sl] = dot_nn(dscores, queries)
            grad_v_ref[0, s0:s1, sl] = dot_nn(weights, grad_raw)


def kept_kernel(
    heads,
    kept_ref,
    core_ref,
    k_ref,
    v_ref,
    intra_k_ref,
    intra_v_ref,
    col_ref,
    later_ref,
    by_head_ref,
    turned_ref,
    grad_k_ref,
    grad_v_ref,
    theirs_ref,
    mine_ref,
    stack,
    turned,
    stack_sem,
    turned_sem,
):
    length = k_ref.shape[1]
    group = pl.program_id(0)
    copies = (
        pltpu.make_async_copy(by_head_ref, stack.at[pl.ds(0, heads)], stack_sem),
        pltpu.make_async_copy(turned_ref, turned, turned_sem),
    )

    @pl.when(group == 0)
    def _():
        for copy in copies:
            copy.start()

    col = col_ref[0]
    tail = jnp.exp(col[length - 1 : length, :] - col)
    for h in range(GROUP):
        sl = head_slice(h)
        later = later_ref[h]
        factor = tail[:, h : h + 1]
        scaled = (k_ref[0, :, sl].astype(F32) * factor).astype(BF16)
        grad_k = intra_k_ref[0, :, sl] + factor * dot_nt(v_ref[0, :, sl], later)
        grad_v = intra_v_ref[0, :, sl] + dot_nn(scaled, later)
        grad_k = grad_k.astype(BF16)
        grad_v = grad_v.astype(BF16)
        grad_k_ref[0, :, sl] = grad_k
        grad_v_ref[0, :, sl] = grad_v
        stack[heads + group * GROUP + h] = grad_k
        stack[2 * heads + group * GROUP + h] = grad_v

    @pl.when(group == pl.num_programs(0) - 1)
    def _():
        for copy in copies:
            copy.wait()
        core = core_ref[0]
        per_row = 3 * heads

        def run(out_ref, parity):
            def body(i, carry):
                number = kept_ref[2 * i + parity]
                left = turned[number // per_row]
                right = stack[lax.rem(number, per_row)]
                out_ref[i] = dot_nn(left, right).astype(BF16)
                return carry

            lax.fori_loop(0, out_ref.shape[0], body, 0, unroll=4)

        run(theirs_ref, 1 - core)
        run(mine_ref, core)


def params(mib):
    return pltpu.CompilerParams(
        dimension_semantics=("arbitrary",), vmem_limit_bytes=mib * MIB
    )


def cost(flops, bytes_accessed, transcendentals=0):
    return pl.CostEstimate(
        flops=flops, bytes_accessed=bytes_accessed, transcendentals=transcendentals
    )


def per_device(
    layer_input, queries, key_vectors, value_vectors, grad_attended, log_decay, kept_blocks
):
    heads = log_decay.shape[1]
    length = queries.shape[1]
    width = queries.shape[2]
    groups = heads // GROUP
    wide = GROUP * BLOCK
    kept = kept_blocks.shape[0]
    seq = ("x", "y")
    blocks = lax.axis_size(seq)
    per_owner = heads // blocks
    rows = per_owner * BLOCK
    pair = GROUP // per_owner

    tokens = pl.BlockSpec((1, length, wide), lambda g, *_: (0, 0, g))
    col_spec = pl.BlockSpec((1, length, GROUP), lambda g, *_: (g, 0, 0))
    row_spec = pl.BlockSpec((1, GROUP, length), lambda g, *_: (g, 0, 0))
    square = pl.BlockSpec((GROUP, BLOCK, BLOCK), lambda g, *_: (g, 0, 0))
    by_head = pl.BlockSpec((GROUP, length, BLOCK), lambda g, *_: (g, 0, 0))
    flat_bf = jax.ShapeDtypeStruct((1, length, width), BF16)
    flat_f32 = jax.ShapeDtypeStruct((1, length, width), F32)
    squares = jax.ShapeDtypeStruct((heads, BLOCK, BLOCK), BF16)
    whole = pl.BlockSpec(memory_space=pltpu.VMEM)
    pairs = heads * length * length

    decay = log_decay[0].reshape(groups, GROUP, length)
    payload, col, row = pl.pallas_call(
        states_kernel,
        grid=(groups,),
        in_specs=[row_spec, tokens, tokens],
        out_specs=[
            pl.BlockSpec((pair, rows + AUX, BLOCK), lambda g: (g, 0, 0)),
            col_spec,
            row_spec,
        ],
        out_shape=[
            jax.ShapeDtypeStruct((blocks, rows + AUX, BLOCK), BF16),
            jax.ShapeDtypeStruct((groups, length, GROUP), F32),
            jax.ShapeDtypeStruct((groups, GROUP, length), F32),
        ],
        compiler_params=params(16),
        name="states",
    )(decay, key_vectors, value_vectors)

    received = lax.all_to_all(payload, seq, 0, 0, tiled=True)

    intra = pl.pallas_call(
        intra_kernel,
        grid=(groups,),
        in_specs=[tokens, tokens, tokens, col_spec, row_spec],
        out_specs=tokens,
        out_shape=flat_f32,
        compiler_params=params(16),
        cost_estimate=cost(pairs * 4 * BLOCK, 6 * length * width * 2, pairs),
        name="intra",
    )(queries, key_vectors, value_vectors, col, row)

    turned = layer_input[0].reshape(length, -1, BLOCK).transpose(1, 2, 0)

    aux = received[:, rows:, :]

    def scan(x, reverse):
        return pl.pallas_call(
            functools.partial(scan_kernel, reverse),
            in_specs=[whole, whole],
            out_specs=whole,
            out_shape=jax.ShapeDtypeStruct((blocks, rows, BLOCK), BF16),
            compiler_params=pltpu.CompilerParams(vmem_limit_bytes=8 * MIB),
            name="scan",
        )(x, aux)

    carried = lax.all_to_all(scan(received, False), seq, 0, 0, tiled=True)
    carried = carried.reshape(heads, BLOCK, BLOCK)

    attended, grad_raw, block_grad = pl.pallas_call(
        norm_kernel,
        grid=(groups,),
        in_specs=[tokens, tokens, tokens, col_spec, square],
        out_specs=[tokens, tokens, square],
        out_shape=[flat_bf, flat_bf, squares],
        compiler_params=params(20),
        name="norm",
    )(intra, queries, grad_attended, col, carried)

    sent = lax.all_to_all(block_grad.reshape(blocks, rows, BLOCK), seq, 0, 0, tiled=True)

    grad_q, grad_q_by_head = pl.pallas_call(
        grad_q_kernel,
        grid=(groups,),
        in_specs=[tokens, tokens, tokens, col_spec, row_spec, square],
        out_specs=[tokens, by_head],
        out_shape=[flat_bf, jax.ShapeDtypeStruct((heads, length, BLOCK), BF16)],
        compiler_params=params(16),
        cost_estimate=cost(pairs * 4 * BLOCK, 6 * length * width * 2, pairs),
        name="grad_q",
    )(grad_raw, key_vectors, value_vectors, col, row, carried)

    later = lax.all_to_all(scan(sent, True), seq, 0, 0, tiled=True)
    later = later.reshape(heads, BLOCK, BLOCK)

    intra_k, intra_v = pl.pallas_call(
        grad_kv_kernel,
        grid=(groups,),
        in_specs=[tokens, tokens, tokens, tokens, col_spec, row_spec],
        out_specs=[tokens, tokens],
        out_shape=[flat_f32, flat_f32],
        compiler_params=params(20),
        cost_estimate=cost(pairs * 8 * BLOCK, 8 * length * width * 2, pairs),
        name="grad_kv",
    )(grad_raw, queries, key_vectors, value_vectors, col, row)

    core = lax.axis_index("core").astype(jnp.int32).reshape(1)
    half = jax.ShapeDtypeStruct((kept // 2, BLOCK, BLOCK), BF16)
    half_spec = pl.BlockSpec((kept // 2, BLOCK, BLOCK), lambda g, *_: (0, 0, 0))
    hbm = pl.BlockSpec(memory_space=pl.ANY)
    grad_k, grad_v, theirs, mine = pl.pallas_call(
        functools.partial(kept_kernel, heads),
        grid_spec=pltpu.PrefetchScalarGridSpec(
            num_scalar_prefetch=2,
            grid=(groups,),
            in_specs=[tokens, tokens, tokens, tokens, col_spec, square, hbm, hbm],
            out_specs=[tokens, tokens, half_spec, half_spec],
            scratch_shapes=[
                pltpu.VMEM((3 * heads, length, BLOCK), BF16),
                pltpu.VMEM(turned.shape, BF16),
                pltpu.SemaphoreType.DMA,
                pltpu.SemaphoreType.DMA,
            ],
        ),
        out_shape=[flat_bf, flat_bf, half, half],
        compiler_params=params(44),
        name="kept",
    )(
        kept_blocks,
        core,
        key_vectors,
        value_vectors,
        intra_k,
        intra_v,
        col,
        later,
        grad_q_by_head,
        turned,
    )

    other = lax.ppermute(theirs, "core", [(0, 1), (1, 0)])
    chip = (mine.astype(F32) + other.astype(F32)).astype(BF16)
    parts = lax.all_to_all(chip, ("x", "y", "z"), 0, 0, tiled=True)
    tokens_all = length * lax.axis_size(("x", "y", "z", "core"))
    grad_blocks = jnp.sum(parts.astype(F32), axis=0, keepdims=True) / math.sqrt(tokens_all)
    return attended, grad_q, grad_k, grad_v, grad_blocks


def solution(mesh):
    physical = Mesh(mesh.devices.reshape(4, 4, 4, 2), ("x", "y", "z", "core"))
    seq, dp = ("x", "y"), ("z", "core")
    tokens = P(dp, seq, None)
    return jax.shard_map(
        per_device,
        mesh=physical,
        in_specs=(tokens, tokens, tokens, tokens, tokens, P(dp, None, seq), P()),
        out_specs=(tokens, tokens, tokens, tokens, P(seq + dp, None, None)),
        check_vma=False,
    )
```

time: 1020 us -> 224 us (0.22); the launches traced: 1010 us -> 223 us
  waiting for transfers between devices: 731 us -> 4.15 us
  matrix products: 121 us -> 0 us
  Pallas kernels: 0 us -> 83.5 us
  blocking collectives: 41.1 us -> 88.1 us
  local copies, waits for them, and re-layouts: 79.6 us -> 35.6 us
  other arithmetic: 20.2 us -> 1.77 us
  between operations: 15 us -> 0.8 us
    reduce_scatter x1 -> x0, waiting for transfers between devices: 615 us -> none  [per_device(): lax.psum_scatter(jnp.einsum('tkr,tkc->krc', input_cols, grad_cols, prefer...]
    dot_general x15 -> x0, matrix products: 121 us -> none  [the longest x1 15.8 us: per_device(): jnp.einsum('nh,nhce->hce', factor, gathered.astype(jnp.float32))]
    all_gather x2 -> x0, waiting for transfers between devices: 116 us -> none  [the longest x1 69.6 us: per_device(): gathered = lax.all_gather(block_grad[None], 'seq', axis=0, tiled=True)]
    all_to_all x0 -> x3, blocking collectives: none -> 88.1 us  [the longest x1 41.1 us: per_device(): parts = lax.all_to_all(chip, ('x', 'y', 'z'), 0, 0, tiled=True)]
    pallas_call x0 -> x8, Pallas kernels: none -> 83.5 us  [the longest x1 19.2 us: per_device(): pl.pallas_call(grad_kv_kernel, grid=(groups,), in_specs=[tokens, tokens,...]
    unnamed x1 -> x0, blocking collectives: 41.1 us -> none
    gather x2 -> x0, local copies, waits for them, and re-layouts: 20.8 us -> none  [the longest x1 10.9 us: per_device(): grad_cols = jnp.take(col_blocks, kept_blocks % per_row, axis=1)]
    another operation x4 -> x0, local copies, waits for them, and re-layouts: 16.4 us -> none  [the longest x1 5.19 us: per_device(): grad_q.reshape(1, length, inner_width)]
  transfers between devices with their start and end apart: 3 -> 3, of which waited for: 3 -> 1; matrix products, arithmetic and copies ran while one was open for 10% -> 3% of each run, Pallas kernels for 0% -> 19%
where the time goes in v1:
time: 224 us; the launch traced here: 223 us
  blocking collectives  88.1 us (39%)
  Pallas kernels  83.5 us (37%)
  local copies, waits for them, and re-layouts  35.6 us (16%)
  starting transfers between devices  8.94 us (4%)
  waiting for transfers between devices  4.15 us (2%)
    all_to_all x1, blocking collectives, per_device(): parts = lax.all_to_all(chip, ('x', 'y', 'z'), 0, 0, tiled=True)  41.1 us
    unnamed x45, local copies, waits for them, and re-layouts  35.5 us
    all_to_all x1, blocking collectives, per_device(): received = lax.all_to_all(payload, seq, 0, 0, tiled=True)  24.8 us
    all_to_all x1, blocking collectives, per_device(): lax.all_to_all(block_grad.reshape(blocks, rows, BLOCK), seq, 0, 0, tiled=...  22.2 us
    pallas_call x1, Pallas kernels, per_device(): pl.pallas_call(grad_kv_kernel, grid=(groups,), in_specs=[tokens, tokens,...  19.2 us
    pallas_call x1, Pallas kernels, per_device(): pl.pallas_call(functools.partial(kept_kernel, heads), grid_spec=pltpu.Pre...  18.9 us
    pallas_call x1, Pallas kernels, per_device(): pl.pallas_call(norm_kernel, grid=(groups,), in_specs=[tokens, tokens, tok...  16 us
    pallas_call x1, Pallas kernels, per_device(): pl.pallas_call(intra_kernel, grid=(groups,), in_specs=[tokens, tokens, to...  12.8 us
  transfers between devices with their start and end apart: 3, of which 1 were waited for; matrix products, arithmetic and copies ran while one was open for 3% of the time, Pallas kernels for 19%

profile of v1, /device:TPU:0, one launch (start us, length us, event | category | flops | bytes accessed | tf_op | source)
XLA Modules:
  0.0 222.8 jit_solution(15681652073374048189)
XLA Ops:
  0.6 0.0 copy-start
  0.6 1.7 copy-done
  2.4 0.0 copy-start.2
  2.4 1.7 copy-done.2
  4.1 0.0 copy-start.20
  4.1 0.8 copy-done.20
  4.9 5.3 %states.1 = (bf16[16,272,128]{2,1,0:T(8,128)(2,1)S(1)}, f32[4,320,8]{2,1,0:T(8,128)S(1)}, f32[4,8,320]{2,1,0:T(8,128)S(1)}) custom-call(f32[4,8,320]{2,1,0:T(8,128)S(1)} %bitcast.11, bf16[1,320,4096]{2,1,0:T(8,128)(2,1)S(1)} %copy-done, bf16[1,320,4096]{2,1,0:T(8,128)(2,1)S(1)} %copy-done.2), custom_call_target="tpu_custom_call" | custom-call | tf_op jit(solution)/shard_map/states/pallas_call | solution.py:269
  10.3 24.8 %all_to_all.25.x_ref = bf16[16,272,128]{2,1,0:T(8,128)(2,1)S(1)} all-to-all(bf16[16,272,128]{2,1,0:T(8,128)(2,1)S(1)} %get-tuple-element.21), channel_id=1, replica_groups=mesh['x'=4,'y'=4,'z'=4,'core'=2] {'x','y'}, dimensions={0} | all-to-all | bytes 2228224 | tf_op jit(solution)/shard_map/all_to_all | solution.py:287
  35.1 0.0 copy-start.1
  35.1 0.2 scan.2
  35.4 0.0 copy-start.14
  35.4 1.0 copy-done.14
  36.3 4.3 %all-to-all-start.1 = ((bf16[16,256,128]{2,1,0:T(8,128)(2,1)}), bf16[16,256,128]{2,1,0:T(8,128)(2,1)}, u32[]{:S(2)}, u32[]{:S(2)}) async-start(bf16[16,256,128]{2,1,0:T(8,128)(2,1)} %copy-done.14), calls=%async_computation.1 | async-start | bytes 2097152 | tf_op jit(solution)/shard_map/all_to_all | solution.py:314
  40.7 0.0 copy-done.1
  40.7 0.0 copy-start.3
  40.7 1.7 copy-done.3
  42.4 0.0 copy-start.8
  42.4 1.7 copy-done.8
  44.2 12.8 %intra.1.raw_ref = f32[1,320,4096]{2,1,0:T(8,128)S(1)} custom-call(bf16[1,320,4096]{2,1,0:T(8,128)(2,1)S(1)} %copy-done.8, bf16[1,320,4096]{2,1,0:T(8,128)(2,1)S(1)} %copy-done.1, bf16[1,320,4096]{2,1,0:T(8,128)(2,1)S(1)} %copy-done.3, f32[4,320,8]{2,1,0:T(8,128)S(1)} %get-tuple-element.19.col_ref, f32[4,8,320]{2,1,0:T(8,128)S(1)} %get-tuple-element.20.row_ref), custom_call_target="tpu_custom_call" | custom-call | flops 1677721600 | bytes 15728640 | tf_op jit(solution)/shard_map/intra/pallas_call | solution.py:289
  57.0 0.0 copy-start.6
  57.0 2.3 %copy-done.6 = f32[1,320,4096]{2,1,0:T(8,128)} copy-done((f32[1,320,4096]{2,1,0:T(8,128)}, f32[1,320,4096]{2,1,0:T(8,128)S(1)}, u32[]{:S(2)}) %copy-start.6) | copy-done | bytes 5242904
  59.3 0.0 all-to-all-done.1
  59.3 0.0 copy-start.7
  59.4 2.5 %copy-done.7 = f32[1,320,4096]{2,1,0:T(8,128)S(1)} copy-done((f32[1,320,4096]{2,1,0:T(8,128)S(1)}, f32[1,320,4096]{2,1,0:T(8,128)}, u32[]{:S(2)}) %copy-start.7) | copy-done | bytes 5242904
  61.8 0.0 copy-start.9
  61.8 1.7 copy-done.9
  63.6 0.0 copy-start.19
  63.6 1.7 copy-done.19
  65.3 16.0 %norm.1 = (bf16[1,320,4096]{2,1,0:T(8,128)(2,1)}, bf16[1,320,4096]{2,1,0:T(8,128)(2,1)S(1)}, bf16[32,128,128]{2,1,0:T(8,128)(2,1)S(1)}) custom-call(f32[1,320,4096]{2,1,0:T(8,128)S(1)} %copy-done.7, bf16[1,320,4096]{2,1,0:T(8,128)(2,1)S(1)} %copy-done.9, bf16[1,320,4096]{2,1,0:T(8,128)(2,1)S(1)} %copy-done.19, f32[4,320,8]{2,1,0:T(8,128)S(1)} %get-tuple-element.19.col_ref, ...), custom_call_target="tpu_custom_call" | custom-call | tf_op jit(solution)/shard_map/norm/pallas_call | solution.py:317
  81.3 0.0 copy-start.15
  81.3 1.5 copy-done.15
  82.8 22.2 %all_to_all.26.x_ref = bf16[16,256,128]{2,1,0:T(8,128)(2,1)S(1)} all-to-all(bf16[16,256,128]{2,1,0:T(8,128)(2,1)S(1)} %bitcast.10), channel_id=1, replica_groups=mesh['x'=4,'y'=4,'z'=4,'core'=2] {'x','y'}, dimensions={0} | all-to-all | bytes 2097152 | tf_op jit(solution)/shard_map/all_to_all | solution.py:327
  105.0 0.2 scan.3
  105.2 0.0 copy-start.13
  105.2 1.0 copy-done.13
  106.2 4.5 %all-to-all-start.3 = ((bf16[16,256,128]{2,1,0:T(8,128)(2,1)}), bf16[16,256,128]{2,1,0:T(8,128)(2,1)}, u32[]{:S(2)}, u32[]{:S(2)}) async-start(bf16[16,256,128]{2,1,0:T(8,128)(2,1)} %copy-done.13), calls=%async_computation.3 | async-start | bytes 2097152 | tf_op jit(solution)/shard_map/all_to_all | solution.py:340
  110.7 6.4 %copy.12 = bf16[1,320,6144]{1,2,0:T(8,128)(2,1)} copy(bf16[1,320,6144]{2,1,0:T(8,128)(2,1)} %param.7) | data formatting | bytes 7864320 | tf_op args[0]
  117.1 0.0 copy-start.4
  117.1 1.7 copy-done.4
  118.9 0.0 copy-start.16
  118.9 1.7 copy-done.16
  120.6 0.0 copy-start.5
  120.6 0.0 copy-start.10
  120.6 0.0 copy-start.17
  120.6 10.8 %grad_q.1 = (bf16[1,320,4096]{2,1,0:T(8,128)(2,1)}, bf16[32,320,128]{2,1,0:T(8,128)(2,1)S(1)}) custom-call(bf16[1,320,4096]{2,1,0:T(8,128)(2,1)S(1)} %copy-done.16, bf16[1,320,4096]{2,1,0:T(8,128)(2,1)S(1)} %copy-done.1, bf16[1,320,4096]{2,1,0:T(8,128)(2,1)S(1)} %copy-done.4, f32[4,320,8]{2,1,0:T(8,128)S(1)} %get-tuple-element.19.col_ref, ...), custom_call_target="tpu_custom_call" | custom-call | flops 1677721600 | bytes 15728640 | tf_op jit(solution)/shard_map/grad_q/pallas_call | solution.py:329
  131.4 0.0 copy-start.18
  131.4 1.5 copy-done.18
  132.9 0.0 copy-done.5
  132.9 0.0 copy-done.10
  132.9 0.0 copy-done.17
  132.9 0.0 copy-start.21
  132.9 19.2 %grad_kv.1 = (f32[1,320,4096]{2,1,0:T(8,128)S(1)}, f32[1,320,4096]{2,1,0:T(8,128)S(1)}) custom-call(bf16[1,320,4096]{2,1,0:T(8,128)(2,1)S(1)} %copy-done.17, bf16[1,320,4096]{2,1,0:T(8,128)(2,1)S(1)} %copy-done.10, bf16[1,320,4096]{2,1,0:T(8,128)(2,1)S(1)} %copy-done.1, bf16[1,320,4096]{2,1,0:T(8,128)(2,1)S(1)} %copy-done.5, ...), custom_call_target="tpu_custom_call" | custom-call | flops 3355443200 | bytes 20971520 | tf_op jit(solution)/shard_map/grad_kv/pallas_call | solution.py:343
  152.1 0.0 copy-start.11
  152.1 2.3 %copy-done.11 = f32[1,320,4096]{2,1,0:T(8,128)} copy-done((f32[1,320,4096]{2,1,0:T(8,128)}, f32[1,320,4096]{2,1,0:T(8,128)S(1)}, u32[]{:S(2)}) %copy-start.11) | copy-done | bytes 5242904
  154.4 2.4 %copy-done.12 = f32[1,320,4096]{2,1,0:T(8,128)} copy-done((f32[1,320,4096]{2,1,0:T(8,128)}, f32[1,320,4096]{2,1,0:T(8,128)S(1)}, u32[]{:S(2)}) %copy-start.12) | copy-done | bytes 5242904
  156.8 0.0 all-to-all-done.3
  156.8 0.0 copy-done.21
  156.8 18.9 %kept.1 = (bf16[1,320,4096]{2,1,0:T(8,128)(2,1)}, bf16[1,320,4096]{2,1,0:T(8,128)(2,1)}, bf16[64,128,128]{2,1,0:T(8,128)(2,1)S(1)}, bf16[64,128,128]{2,1,0:T(8,128)(2,1)S(1)}) custom-call(s32[128]{0:T(128)S(1)} %copy-done.21, s32[1]{0:T(128)} %bitcast.2.core_ref, bf16[1,320,4096]{2,1,0:T(8,128)(2,1)S(1)} %copy-done.1, bf16[1,320,4096]{2,1,0:T(8,128)(2,1)} %v_ref.9, ...), custom_call_target="tpu_custom_call" | custom-call | tf_op jit(solution)/shard_map/kept/pallas_call | solution.py:358
  175.7 0.1 collective-permute-start
  175.8 4.1 %collective-permute-done = bf16[64,128,128]{2,1,0:T(8,128)(2,1)S(1)} collective-permute-done((bf16[64,128,128]{2,1,0:T(8,128)(2,1)S(1)}, bf16[64,128,128]{2,1,0:T(8,128)(2,1)S(1)}, u32[]{:S(2)}, u32[]{:S(2)}) %collective-permute-start) | collective-permute-done | bytes 2097184 | tf_op jit(solution)/shard_map/ppermute | solution.py:388
  180.0 0.8 add_convert_fusion
  180.8 41.1 %all_to_all.27 = bf16[64,128,128]{2,1,0:T(8,128)(2,1)S(1)} all-to-all(bf16[64,128,128]{2,1,0:T(8,128)(2,1)S(1)} %add_convert_fusion), channel_id=1, replica_groups=mesh['x'=4,'y'=4,'z'=4,'core'=2] {'x','y','z'}, dimensions={0} | all-to-all | bytes 4194304 | tf_op jit(solution)/shard_map/all_to_all | solution.py:390
  221.9 0.3 convert_reduce_fusion
  222.2 0.6 multiply_bitcast_fusion
  (2 shorter events, 0.0 us)
Async XLA Ops:
  0.6 1.7 copy-start
  2.4 1.7 copy-start.2
  4.1 0.8 copy-start.20
  35.1 5.6 %copy-start.1 = (bf16[1,320,4096]{2,1,0:T(8,128)(2,1)S(1)}, bf16[1,320,4096]{2,1,0:T(8,128)(2,1)}, u32[]{:S(2)}) copy-start(bf16[1,320,4096]{2,1,0:T(8,128)(2,1)} %k_ref.9) | copy-start | bytes 7864324
  35.4 1.0 copy-start.14
  36.3 23.0 %all-to-all-start.1 = ((bf16[16,256,128]{2,1,0:T(8,128)(2,1)}), bf16[16,256,128]{2,1,0:T(8,128)(2,1)}, u32[]{:S(2)}, u32[]{:S(2)}) async-start(bf16[16,256,128]{2,1,0:T(8,128)(2,1)} %copy-done.14), calls=%async_computation.1 | async-start | bytes 2097152 | tf_op jit(solution)/shard_map/all_to_all | solution.py:314
  40.7 1.7 copy-start.3
  42.4 1.7 copy-start.8
  57.0 2.3 %copy-start.6 = (f32[1,320,4096]{2,1,0:T(8,128)}, f32[1,320,4096]{2,1,0:T(8,128)S(1)}, u32[]{:S(2)}) copy-start(f32[1,320,4096]{2,1,0:T(8,128)S(1)} %intra.1.raw_ref) | copy-start | bytes 15728644
  59.3 2.5 %copy-start.7 = (f32[1,320,4096]{2,1,0:T(8,128)S(1)}, f32[1,320,4096]{2,1,0:T(8,128)}, u32[]{:S(2)}) copy-start(f32[1,320,4096]{2,1,0:T(8,128)} %copy-done.6) | copy-start | bytes 15728644
  61.8 1.7 copy-start.9
  63.6 1.7 copy-start.19
  81.3 1.5 copy-start.15
  105.2 1.0 copy-start.13
  106.2 50.6 %all-to-all-start.3 = ((bf16[16,256,128]{2,1,0:T(8,128)(2,1)}), bf16[16,256,128]{2,1,0:T(8,128)(2,1)}, u32[]{:S(2)}, u32[]{:S(2)}) async-start(bf16[16,256,128]{2,1,0:T(8,128)(2,1)} %copy-done.13), calls=%async_computation.3 | async-start | bytes 2097152 | tf_op jit(solution)/shard_map/all_to_all | solution.py:340
  117.1 1.7 copy-start.4
  118.9 1.7 copy-start.16
  120.6 12.3 %copy-start.5 = (bf16[1,320,4096]{2,1,0:T(8,128)(2,1)S(1)}, bf16[1,320,4096]{2,1,0:T(8,128)(2,1)}, u32[]{:S(2)}) copy-start(bf16[1,320,4096]{2,1,0:T(8,128)(2,1)} %v_ref.9) | copy-start | bytes 7864324
  120.6 12.3 %copy-start.10 = (bf16[1,320,4096]{2,1,0:T(8,128)(2,1)S(1)}, bf16[1,320,4096]{2,1,0:T(8,128)(2,1)}, u32[]{:S(2)}) copy-start(bf16[1,320,4096]{2,1,0:T(8,128)(2,1)} %q_ref.5) | copy-start | bytes 7864324
  120.6 12.3 %copy-start.17 = (bf16[1,320,4096]{2,1,0:T(8,128)(2,1)S(1)}, bf16[1,320,4096]{2,1,0:T(8,128)(2,1)}, u32[]{:S(2)}) copy-start(bf16[1,320,4096]{2,1,0:T(8,128)(2,1)} %copy-done.15) | copy-start | bytes 7864324
  131.4 1.5 copy-start.18
  132.9 23.9 %copy-start.21 = (s32[128]{0:T(128)S(1)}, s32[128]{0:T(128)}, u32[]{:S(2)}) copy-start(s32[128]{0:T(128)} %kept_ref.1) | copy-start | bytes 1540
  152.1 2.3 %copy-start.11 = (f32[1,320,4096]{2,1,0:T(8,128)}, f32[1,320,4096]{2,1,0:T(8,128)S(1)}, u32[]{:S(2)}) copy-start(f32[1,320,4096]{2,1,0:T(8,128)S(1)} %get-tuple-element.25.intra_k_ref) | copy-start | bytes 15728644
  154.4 2.4 %copy-start.12 = (f32[1,320,4096]{2,1,0:T(8,128)}, f32[1,320,4096]{2,1,0:T(8,128)S(1)}, u32[]{:S(2)}) copy-start(f32[1,320,4096]{2,1,0:T(8,128)S(1)} %get-tuple-element.26.intra_v_ref) | copy-start | bytes 15728644
  175.7 4.2 %collective-permute-start = (bf16[64,128,128]{2,1,0:T(8,128)(2,1)S(1)}, bf16[64,128,128]{2,1,0:T(8,128)(2,1)S(1)}, u32[]{:S(2)}, u32[]{:S(2)}) collective-permute-start(bf16[64,128,128]{2,1,0:T(8,128)(2,1)S(1)} %get-tuple-element.32), channel_id=1, source_target_pairs={{0,1},{1,0},{2,3},{3,2},{4,5},{5,4},{6,7},{7,6},{8,9},{9,8},{10,11... | collective-permute-start | bytes 6291464 | tf_op jit(solution)/shard_map/ppermute | solution.py:388

commit v2 on v1

v2 whole, which is shorter than its diff:
```python
import functools
import math

import jax
import jax.numpy as jnp
from jax import lax
from jax.experimental import pallas as pl
from jax.experimental.pallas import tpu as pltpu
from jax.sharding import Mesh
from jax.sharding import PartitionSpec as P

BLOCK = 128
GROUP = 8
WIDE = 256
KEPT_UNROLL = 16
AUX = 16
F32 = jnp.float32
BF16 = jnp.bfloat16
MIB = 1 << 20


def dot_nt(a, b):
    return lax.dot_general(a, b, (((1,), (1,)), ((), ())), preferred_element_type=F32)


def dot_nn(a, b):
    return lax.dot_general(a, b, (((1,), (0,)), ((), ())), preferred_element_type=F32)


def dot_tn(a, b):
    return lax.dot_general(a, b, (((0,), (0,)), ((), ())), preferred_element_type=F32)


def head_slice(h):
    return slice(h * BLOCK, (h + 1) * BLOCK)


def batches(size):
    return [range(h, h + size) for h in range(0, GROUP, size)]


def states_kernel(decay_ref, k_ref, v_ref, payload_ref, col_ref, row_ref):
    length = k_ref.shape[1]
    group = pl.program_id(0)
    groups = col_ref.shape[0]
    heads = groups * GROUP

    @pl.when(group == 0)
    def _():
        decay = decay_ref[...]
        high = decay.astype(BF16).astype(F32)
        rest = decay - high
        middle = rest.astype(BF16).astype(F32)
        terms = jnp.concatenate([high, middle, rest - middle], axis=0).astype(BF16)
        t = lax.broadcasted_iota(jnp.int32, (length, length), 0)
        s = lax.broadcasted_iota(jnp.int32, (length, length), 1)
        lower = jnp.where(s <= t, 1.0, 0.0).astype(BF16)
        upper = jnp.where(t <= s, 1.0, 0.0).astype(BF16)
        cols = dot_nt(lower, terms)
        rows = dot_nn(terms, upper)
        row = rows[:heads] + rows[heads : 2 * heads] + rows[2 * heads :]
        for g in range(groups):
            at = [slice(n * heads + g * GROUP, n * heads + (g + 1) * GROUP) for n in range(3)]
            col_ref[g] = cols[:, at[0]] + cols[:, at[1]] + cols[:, at[2]]
            row_ref[g] = row[g * GROUP : (g + 1) * GROUP]

    col = col_ref[group]
    total = col[length - 1 : length, :]
    tail = jnp.exp(total - col)
    whole = jnp.exp(total)
    index = lax.broadcasted_iota(jnp.int32, (AUX, BLOCK), 0)
    for hs in batches(4):
        scaled = [v_ref[0, :, head_slice(h)].astype(F32) * tail[:, h : h + 1] for h in hs]
        states = [dot_tn(k_ref[0, :, head_slice(h)], x.astype(BF16)) for h, x in zip(hs, scaled)]
        for h, state in zip(hs, states):
            payload_ref[h // 2, head_slice(h % 2), :] = state.astype(BF16)
    for p in range(GROUP // 2):
        aux = jnp.zeros((AUX, BLOCK), F32)
        for i in range(2):
            value = jnp.broadcast_to(whole[:, 2 * p + i : 2 * p + i + 1], (AUX, BLOCK))
            first = value.astype(BF16).astype(F32)
            aux = jnp.where(index == 2 * i, first, aux)
            aux = jnp.where(index == 2 * i + 1, value - first, aux)
        payload_ref[p, 2 * BLOCK :, :] = aux.astype(BF16)


def first_scan_kernel(x_ref, after_ref, out_ref, whole_ref):
    del after_ref
    blocks = x_ref.shape[0]
    running = [jnp.zeros((BLOCK, BLOCK), F32) for _ in range(2)]
    for j in range(blocks):
        aux = x_ref[j, 2 * BLOCK :, :].astype(F32)
        for i in range(2):
            out_ref[j, head_slice(i), :] = running[i].astype(BF16)
            whole = aux[2 * i : 2 * i + 1] + aux[2 * i + 1 : 2 * i + 2]
            whole_ref[j, i : i + 1, :] = whole
            running[i] = running[i] * whole + x_ref[j, head_slice(i), :].astype(F32)


def second_scan_kernel(x_ref, whole_ref, after_ref, out_ref):
    del after_ref
    blocks = x_ref.shape[0]
    running = [jnp.zeros((BLOCK, BLOCK), F32) for _ in range(2)]
    for j in range(blocks - 1, -1, -1):
        for i in range(2):
            out_ref[j, head_slice(i), :] = running[i].astype(BF16)
            whole = whole_ref[j, i : i + 1, :]
            running[i] = running[i] * whole + x_ref[j, head_slice(i), :].astype(F32)


def within(gap, offset):
    t = lax.broadcasted_iota(jnp.int32, gap.shape, 0)
    s = lax.broadcasted_iota(jnp.int32, gap.shape, 1) + offset
    return jnp.where(s <= t, jnp.exp(gap), 0.0)


def intra_kernel(q_ref, k_ref, v_ref, col_ref, row_ref, raw_ref, scaled_ref):
    col = col_ref[0]
    head_decay = jnp.exp(col)
    for hs in batches(2):
        parts = []
        for h in hs:
            sl = head_slice(h)
            at = slice(h, h + 1)
            scores = dot_nt(q_ref[0, :, sl], k_ref[0, :WIDE, sl])
            weights = scores * within(col[:, at] - row_ref[0, at, :WIDE], 0)
            scores = dot_nt(q_ref[0, WIDE:, sl], k_ref[0, WIDE:, sl])
            gap = col[WIDE:, at] - row_ref[0, at, WIDE:]
            parts.append((weights.astype(BF16), (scores * within(gap, 0)).astype(BF16)))
        for h, (weights, last) in zip(hs, parts):
            sl = head_slice(h)
            raw = dot_nn(weights, v_ref[0, :WIDE, sl])
            end = raw[WIDE:] + dot_nn(last, v_ref[0, WIDE:, sl])
            raw_ref[0, :WIDE, sl] = raw[:WIDE]
            raw_ref[0, WIDE:, sl] = end
            queries = q_ref[0, :, sl].astype(F32)
            scaled_ref[0, :, sl] = (queries * head_decay[:, h : h + 1]).astype(BF16)


def turn_kernel(x_ref, out_ref):
    for n in range(out_ref.shape[0]):
        out_ref[n] = x_ref[0, :, head_slice(n)].T


def norm_kernel(
    raw_ref, scaled_ref, g_ref, carried_ref, attended_ref, grad_raw_ref, grad_ref
):
    for hs in batches(8):
        sls = [head_slice(h) for h in hs]
        raws = [dot_nn(scaled_ref[0, :, sl], carried_ref[h]) for h, sl in zip(hs, sls)]
        raws = [raw + raw_ref[0, :, sl] for raw, sl in zip(raws, sls)]
        squares = [jnp.mean(raw * raw, axis=1, keepdims=True) for raw in raws]
        shareds = [
            jnp.mean(g_ref[0, :, sl].astype(F32) * raw, axis=1, keepdims=True)
            for raw, sl in zip(raws, sls)
        ]
        inverses = [lax.rsqrt(square + 1e-6) for square in squares]
        grads = []
        for raw, inverse, shared, sl in zip(raws, inverses, shareds, sls):
            normed = raw * inverse
            attended_ref[0, :, sl] = normed.astype(BF16)
            upstream = g_ref[0, :, sl].astype(F32)
            grad_raw = (inverse * (upstream - normed * (shared * inverse))).astype(BF16)
            grad_raw_ref[0, :, sl] = grad_raw
            grads.append(grad_raw)
        for h, sl, grad_raw in zip(hs, sls, grads):
            grad_ref[h] = dot_tn(scaled_ref[0, :, sl], grad_raw).astype(BF16)


def grad_q_kernel(
    grad_raw_ref,
    k_ref,
    v_ref,
    col_ref,
    row_ref,
    carried_ref,
    grad_q_ref,
    by_head_ref,
):
    col = col_ref[0]
    head_decay = jnp.exp(col)
    for hs in batches(2):
        parts = []
        for h in hs:
            sl = head_slice(h)
            at = slice(h, h + 1)
            scores = dot_nt(grad_raw_ref[0, :, sl], v_ref[0, :WIDE, sl])
            dscores = scores * within(col[:, at] - row_ref[0, at, :WIDE], 0)
            scores = dot_nt(grad_raw_ref[0, WIDE:, sl], v_ref[0, WIDE:, sl])
            gap = col[WIDE:, at] - row_ref[0, at, WIDE:]
            parts.append((dscores.astype(BF16), (scores * within(gap, 0)).astype(BF16)))
        for h, (dscores, last) in zip(hs, parts):
            sl = head_slice(h)
            carried = dot_nt(grad_raw_ref[0, :, sl], carried_ref[h])
            grad_q = dot_nn(dscores, k_ref[0, :WIDE, sl]) + head_decay[:, h : h + 1] * carried
            end = grad_q[WIDE:] + dot_nn(last, k_ref[0, WIDE:, sl])
            for cut, part in ((slice(0, WIDE), grad_q[:WIDE]), (slice(WIDE, None), end)):
                part = part.astype(BF16)
                grad_q_ref[0, cut, sl] = part
                by_head_ref[h, cut, :] = part


def grad_kv_kernel(
    grad_raw_ref,
    q_ref,
    k_ref,
    v_ref,
    col_ref,
    row_ref,
    grad_k_ref,
    grad_v_ref,
    scaled_k_ref,
    scaled_v_ref,
):
    length = k_ref.shape[1]
    col = col_ref[0]
    tail = jnp.exp(col[length - 1 : length, :] - col)
    split = length - WIDE

    def turned_within(h, rows, start, stop):
        gap = row_ref[0, h : h + 1, start:stop] - col[:rows, h : h + 1]
        s = lax.broadcasted_iota(jnp.int32, gap.shape, 0)
        t = lax.broadcasted_iota(jnp.int32, gap.shape, 1) + start
        return jnp.where(s <= t, jnp.exp(gap), 0.0)

    for hs in batches(2):
        parts = []
        for h in hs:
            sl = head_slice(h)
            near = turned_within(h, length, split, length)
            first = turned_within(h, split, 0, split)
            parts.append(
                [
                    (dot_nt(k_ref[0, :, sl], q_ref[0, split:, sl]) * near).astype(BF16),
                    (dot_nt(v_ref[0, :, sl], grad_raw_ref[0, split:, sl]) * near).astype(BF16),
                    (dot_nt(k_ref[0, :split, sl], q_ref[0, :split, sl]) * first).astype(BF16),
                    (dot_nt(v_ref[0, :split, sl], grad_raw_ref[0, :split, sl]) * first).astype(BF16),
                ]
            )
        for h, (weights, dscores, first_weights, first_dscores) in zip(hs, parts):
            sl = head_slice(h)
            grad_k = dot_nn(dscores, q_ref[0, split:, sl])
            grad_v = dot_nn(weights, grad_raw_ref[0, split:, sl])
            first_k = grad_k[:split] + dot_nn(first_dscores, q_ref[0, :split, sl])
            first_v = grad_v[:split] + dot_nn(first_weights, grad_raw_ref[0, :split, sl])
            grad_k_ref[0, :split, sl] = first_k.astype(BF16)
            grad_k_ref[0, split:, sl] = grad_k[split:].astype(BF16)
            grad_v_ref[0, :split, sl] = first_v.astype(BF16)
            grad_v_ref[0, split:, sl] = grad_v[split:].astype(BF16)
            factor = tail[:, h : h + 1]
            scaled_k_ref[0, :, sl] = (k_ref[0, :, sl].astype(F32) * factor).astype(BF16)
            scaled_v_ref[0, :, sl] = (v_ref[0, :, sl].astype(F32) * factor).astype(BF16)


def kept_kernel(
    heads,
    kept_ref,
    core_ref,
    scaled_k_ref,
    scaled_v_ref,
    intra_k_ref,
    intra_v_ref,
    later_ref,
    by_head_ref,
    turned_ref,
    grad_k_ref,
    grad_v_ref,
    theirs_ref,
    mine_ref,
    stack,
    turned,
    stack_sem,
    turned_sem,
):
    group = pl.program_id(0)
    copies = (
        pltpu.make_async_copy(by_head_ref, stack.at[pl.ds(0, heads)], stack_sem),
        pltpu.make_async_copy(turned_ref, turned, turned_sem),
    )

    @pl.when(group == 0)
    def _():
        for copy in copies:
            copy.start()

    for hs in batches(4):
        sls = [head_slice(h) for h in hs]
        grads_k = [dot_nt(scaled_v_ref[0, :, sl], later_ref[h]) for h, sl in zip(hs, sls)]
        grads_v = [dot_nn(scaled_k_ref[0, :, sl], later_ref[h]) for h, sl in zip(hs, sls)]
        for h, sl, grad_k, grad_v in zip(hs, sls, grads_k, grads_v):
            grad_k = (intra_k_ref[0, :, sl].astype(F32) + grad_k).astype(BF16)
            grad_v = (intra_v_ref[0, :, sl].astype(F32) + grad_v).astype(BF16)
            grad_k_ref[0, :, sl] = grad_k
            grad_v_ref[0, :, sl] = grad_v
            stack[heads + group * GROUP + h] = grad_k
            stack[2 * heads + group * GROUP + h] = grad_v

    @pl.when(group == pl.num_programs(0) - 1)
    def _():
        for copy in copies:
            copy.wait()
        core = core_ref[0]
        per_row = 3 * heads

        def run(out_ref, parity):
            def body(i, carry):
                number = kept_ref[2 * i + parity]
                left = turned[number // per_row]
                right = stack[lax.rem(number, per_row)]
                out_ref[i] = dot_nn(left, right).astype(BF16)
                return carry

            lax.fori_loop(0, out_ref.shape[0], body, 0, unroll=KEPT_UNROLL)

        run(theirs_ref, 1 - core)
        run(mine_ref, core)


def in_hbm(x):
    return pltpu.with_memory_space_constraint(x, pltpu.HBM)


def in_vmem(x):
    return pltpu.with_memory_space_constraint(x, pltpu.VMEM)


def call(name, kernel, grid, in_specs, out_specs, out_shape, mib, work=None, prefetch=0, scratch=()):
    estimate = None
    if work is not None:
        estimate = pl.CostEstimate(flops=work[0], bytes_accessed=work[1], transcendentals=0)
    return pl.pallas_call(
        kernel,
        grid_spec=pltpu.PrefetchScalarGridSpec(
            num_scalar_prefetch=prefetch,
            grid=grid,
            in_specs=in_specs,
            out_specs=out_specs,
            scratch_shapes=scratch,
        ),
        out_shape=out_shape,
        compiler_params=pltpu.CompilerParams(
            dimension_semantics=("arbitrary",) * len(grid), vmem_limit_bytes=mib * MIB
        ),
        cost_estimate=estimate,
        name=name,
    )


def per_device(
    layer_input, queries, key_vectors, value_vectors, grad_attended, log_decay, kept_blocks
):
    heads = log_decay.shape[1]
    length = queries.shape[1]
    width = queries.shape[2]
    groups = heads // GROUP
    wide = GROUP * BLOCK
    kept = kept_blocks.shape[0]
    seq = ("x", "y")
    blocks = lax.axis_size(seq)
    per_owner = heads // blocks
    rows = per_owner * BLOCK
    pair = GROUP // per_owner
    row_blocks = layer_input.shape[2] // BLOCK

    tokens = pl.BlockSpec((1, length, wide), lambda g, *_: (0, 0, g))
    col_spec = pl.BlockSpec((1, length, GROUP), lambda g, *_: (g, 0, 0))
    row_spec = pl.BlockSpec((1, GROUP, length), lambda g, *_: (g, 0, 0))
    square = pl.BlockSpec((GROUP, BLOCK, BLOCK), lambda g, *_: (g, 0, 0))
    by_head = pl.BlockSpec((GROUP, length, BLOCK), lambda g, *_: (g, 0, 0))
    flat = (1, length, width)
    head_major = (heads, length, BLOCK)
    whole = pl.BlockSpec(memory_space=pltpu.VMEM)
    anywhere = pl.BlockSpec(memory_space=pl.ANY)
    pairs = heads * length * length
    hbm, vmem = pltpu.HBM, pltpu.VMEM

    def at_start(*shape):
        return pl.BlockSpec(shape, lambda g, *_: (0,) * len(shape))

    queries, key_vectors, value_vectors = map(in_hbm, (queries, key_vectors, value_vectors))
    grad_attended, layer_input = in_hbm(grad_attended), in_hbm(layer_input)
    decay = in_hbm(log_decay[0])

    payload, col, row = call(
        "states",
        states_kernel,
        (groups,),
        [at_start(heads, length), tokens, tokens],
        [
            pl.BlockSpec((pair, rows + AUX, BLOCK), lambda g: (g, 0, 0)),
            at_start(groups, length, GROUP),
            at_start(groups, GROUP, length),
        ],
        [
            vmem((blocks, rows + AUX, BLOCK), BF16),
            vmem((groups, length, GROUP), F32),
            vmem((groups, GROUP, length), F32),
        ],
        16,
    )(decay, key_vectors, value_vectors)
    col, row = in_vmem(col), in_vmem(row)

    received = lax.all_to_all(payload, seq, 0, 0, tiled=True)

    turned = in_hbm(
        call(
            "turn",
            turn_kernel,
            (6,),
            [pl.BlockSpec((1, length, row_blocks * BLOCK // 6), lambda g: (0, 0, g))],
            pl.BlockSpec((row_blocks // 6, BLOCK, length), lambda g: (g, 0, 0)),
            hbm((row_blocks, BLOCK, length), BF16),
            32,
            (pairs * 2 * BLOCK, 2 * length * row_blocks * BLOCK * 2),
        )(layer_input)
    )

    scanned, whole_decay = call(
        "first_scan",
        first_scan_kernel,
        (),
        [whole, anywhere],
        [whole, whole],
        [vmem((blocks, rows, BLOCK), BF16), vmem((blocks, 8, BLOCK), F32)],
        8,
    )(in_vmem(received), turned)
    carried = lax.all_to_all(scanned, seq, 0, 0, tiled=True)
    carried = in_vmem(carried.reshape(heads, BLOCK, BLOCK))

    intra, scaled_q = call(
        "intra",
        intra_kernel,
        (groups,),
        [tokens, tokens, tokens, col_spec, row_spec],
        [tokens, tokens],
        [hbm(flat, F32), hbm(flat, BF16)],
        32,
        (pairs * 4 * BLOCK, 9 * length * width * 2),
    )(queries, key_vectors, value_vectors, col, row)
    intra, scaled_q = in_hbm(intra), in_hbm(scaled_q)

    attended, grad_raw, block_grad = call(
        "norm",
        norm_kernel,
        (groups,),
        [tokens, tokens, tokens, square],
        [tokens, tokens, square],
        [hbm(flat, BF16), hbm(flat, BF16), vmem((heads, BLOCK, BLOCK), BF16)],
        32,
    )(intra, scaled_q, grad_attended, carried)
    grad_raw = in_hbm(grad_raw)

    sent = lax.all_to_all(block_grad.reshape(blocks, rows, BLOCK), seq, 0, 0, tiled=True)

    grad_q, grad_q_by_head = call(
        "grad_q",
        grad_q_kernel,
        (groups,),
        [tokens, tokens, tokens, col_spec, row_spec, square],
        [tokens, by_head],
        [hbm(flat, BF16), hbm(head_major, BF16)],
        32,
        (pairs * 4 * BLOCK, 6 * length * width * 2),
    )(grad_raw, key_vectors, value_vectors, col, row, carried)
    grad_q_by_head = in_hbm(grad_q_by_head)

    scanned = call(
        "second_scan",
        second_scan_kernel,
        (),
        [whole, whole, anywhere],
        whole,
        vmem((blocks, rows, BLOCK), BF16),
        8,
    )(in_vmem(sent), in_vmem(whole_decay), grad_q_by_head)
    later = lax.all_to_all(scanned, seq, 0, 0, tiled=True)
    later = in_vmem(later.reshape(heads, BLOCK, BLOCK))

    intra_k, intra_v, scaled_k, scaled_v = call(
        "grad_kv",
        grad_kv_kernel,
        (groups,),
        [tokens, tokens, tokens, tokens, col_spec, row_spec],
        [tokens] * 4,
        [hbm(flat, BF16)] * 4,
        32,
        (pairs * 8 * BLOCK, 8 * length * width * 2),
    )(grad_raw, queries, key_vectors, value_vectors, col, row)
    intra_k, intra_v, scaled_k, scaled_v = map(in_hbm, (intra_k, intra_v, scaled_k, scaled_v))

    core = lax.axis_index("core").astype(jnp.int32).reshape(1)
    half = (kept // 2, BLOCK, BLOCK)
    grad_k, grad_v, theirs, mine = call(
        "kept",
        functools.partial(kept_kernel, heads),
        (groups,),
        [tokens, tokens, tokens, tokens, square, anywhere, anywhere],
        [tokens, tokens, at_start(*half), at_start(*half)],
        [hbm(flat, BF16), hbm(flat, BF16), vmem(half, BF16), vmem(half, BF16)],
        44,
        prefetch=2,
        scratch=[
            pltpu.VMEM((3 * heads, length, BLOCK), BF16),
            pltpu.VMEM(turned.shape, BF16),
            pltpu.SemaphoreType.DMA,
            pltpu.SemaphoreType.DMA,
        ],
    )(
        kept_blocks,
        core,
        scaled_k,
        scaled_v,
        intra_k,
        intra_v,
        later,
        grad_q_by_head,
        turned,
    )

    other = lax.ppermute(theirs, "core", [(0, 1), (1, 0)])
    chip = (mine.astype(F32) + other.astype(F32)).astype(BF16)
    parts = lax.all_to_all(chip, ("x", "y", "z"), 0, 0, tiled=True)
    tokens_all = length * lax.axis_size(("x", "y", "z", "core"))
    grad_blocks = jnp.sum(parts.astype(F32), axis=0, keepdims=True) / math.sqrt(tokens_all)
    return attended, grad_q, grad_k, grad_v, grad_blocks


def solution(mesh):
    physical = Mesh(mesh.devices.reshape(4, 4, 4, 2), ("x", "y", "z", "core"))
    seq, dp = ("x", "y"), ("z", "core")
    tokens = P(dp, seq, None)
    return jax.shard_map(
        per_device,
        mesh=physical,
        in_specs=(tokens, tokens, tokens, tokens, tokens, P(dp, None, seq), P()),
        out_specs=(tokens, tokens, tokens, tokens, P(seq + dp, None, None)),
        check_vma=False,
    )
```

time: 224 us -> 163 us (0.73)
  blocking collectives: 88.1 us -> 39.7 us
  local copies, waits for them, and re-layouts: 35.6 us -> 2.93 us
  waiting for transfers between devices: 4.15 us -> 31.4 us
  Pallas kernels: 83.5 us -> 67.6 us
  starting transfers between devices: 8.94 us -> 18.2 us
    all_to_all x2 -> x0, blocking collectives: 47 us -> none  [the longest x1 24.8 us: per_device(): received = lax.all_to_all(payload, seq, 0, 0, tiled=True)]
    unnamed x45 -> x8, local copies, waits for them, and re-layouts: 35.5 us -> 2.93 us
    all_to_all x2 -> x4, waiting for transfers between devices: 0.01 us -> 27.2 us  [the longest x1 12.1 us: per_device(): received = lax.all_to_all(payload, seq, 0, 0, tiled=True)]
    pallas_call x8 -> x9, Pallas kernels: 83.5 us -> 67.6 us  [the longest x1 14.1 us: per_device(): call('grad_kv', grad_kv_kernel, (groups,), [tokens, tokens, tokens, token...]
    all_to_all x2 -> x4, starting transfers between devices: 8.86 us -> 18.1 us  [the longest x1 7.12 us: per_device(): received = lax.all_to_all(payload, seq, 0, 0, tiled=True)]
  transfers between devices with their start and end apart: 3 -> 5, of which waited for: 1 -> 5; matrix products, arithmetic and copies ran while one was open for 3% -> 0% of each run, Pallas kernels for 19% -> 23%
where the time goes in v2:
time: 163 us; the launch traced here: 162 us
  Pallas kernels  67.6 us (41%)
  blocking collectives  39.7 us (24%)
  waiting for transfers between devices  31.4 us (19%)
  starting transfers between devices  18.2 us (11%)
  local copies, waits for them, and re-layouts  2.93 us (2%)
  other arithmetic  1.77 us (1%)
    all_to_all x1, blocking collectives, per_device(): parts = lax.all_to_all(chip, ('x', 'y', 'z'), 0, 0, tiled=True)  39.7 us
    pallas_call x1, Pallas kernels, per_device(): call('grad_kv', grad_kv_kernel, (groups,), [tokens, tokens, tokens, token...  14.1 us
    pallas_call x1, Pallas kernels, per_device(): call('kept', functools.partial(kept_kernel, heads), (groups,), [tokens, t...  14 us
    all_to_all x1, waiting for transfers between devices, per_device(): received = lax.all_to_all(payload, seq, 0, 0, tiled=True)  12.1 us
    pallas_call x1, Pallas kernels, per_device(): call('grad_q', grad_q_kernel, (groups,), [tokens, tokens, tokens, col_spe...  8.96 us
    pallas_call x1, Pallas kernels, per_device(): call('intra', intra_kernel, (groups,), [tokens, tokens, tokens, col_spec,...  8.62 us
    pallas_call x1, Pallas kernels, per_device(): call('norm', norm_kernel, (groups,), [tokens, tokens, tokens, square], [t...  8.41 us
    all_to_all x1, starting transfers between devices, per_device(): received = lax.all_to_all(payload, seq, 0, 0, tiled=True)  7.12 us
  transfers between devices with their start and end apart: 5, of which 5 were waited for; matrix products, arithmetic and copies ran while one was open for 0% of the time, Pallas kernels for 23%

profile of v2, /device:TPU:0, one launch (start us, length us, event | category | flops | bytes accessed | tf_op | source)
XLA Modules:
  0.0 162.3 jit_solution(6371706549824789882)
XLA Ops:
  0.6 5.7 %states.1 = (bf16[16,272,128]{2,1,0:T(8,128)(2,1)S(1)}, f32[4,320,8]{2,1,0:T(8,128)S(1)}, f32[4,8,320]{2,1,0:T(8,128)S(1)}) custom-call(f32[32,320]{1,0:T(8,128)} %bitcast.11, bf16[1,320,4096]{2,1,0:T(8,128)(2,1)} %k_ref.7, bf16[1,320,4096]{2,1,0:T(8,128)(2,1)} %v_ref.7), custom_call_target="tpu_custom_call" | custom-call | tf_op jit(solution)/shard_map/states/pallas_call | solution.py:384
  6.3 0.0 copy-start
  6.3 1.0 copy-done
  7.3 7.1 %all-to-all-start = ((bf16[16,272,128]{2,1,0:T(8,128)(2,1)}), bf16[16,272,128]{2,1,0:T(8,128)(2,1)S(1)}, u32[]{:S(2)}, u32[]{:S(2)}) async-start(bf16[16,272,128]{2,1,0:T(8,128)(2,1)} %copy-done), calls=%async_computation | async-start | bytes 2228224 | tf_op jit(solution)/shard_map/all_to_all | solution.py:403
  14.4 6.4 %turn.1.after_ref.turned_ref = bf16[48,128,320]{2,1,0:T(8,128)(2,1)} custom-call(bf16[1,320,6144]{2,1,0:T(8,128)(2,1)} %x_ref.1), custom_call_target="tpu_custom_call" | custom-call | flops 838860800 | bytes 7864320 | tf_op jit(solution)/shard_map/turn/pallas_call | solution.py:406
  20.8 12.1 %all-to-all-done.x_ref = bf16[16,272,128]{2,1,0:T(8,128)(2,1)S(1)} async-done(((bf16[16,272,128]{2,1,0:T(8,128)(2,1)}), bf16[16,272,128]{2,1,0:T(8,128)(2,1)S(1)}, u32[]{:S(2)}, u32[]{:S(2)}) %all-to-all-start) | async-done | bytes 1114144 | tf_op jit(solution)/shard_map/all_to_all | solution.py:403
  32.9 0.2 first_scan.1
  33.2 0.0 copy-start.2
  33.2 1.0 copy-done.2
  34.2 3.7 %all-to-all-start.1 = ((bf16[16,256,128]{2,1,0:T(8,128)(2,1)}), bf16[16,256,128]{2,1,0:T(8,128)(2,1)S(1)}, u32[]{:S(2)}, u32[]{:S(2)}) async-start(bf16[16,256,128]{2,1,0:T(8,128)(2,1)} %copy-done.2), calls=%async_computation.1 | async-start | bytes 2097152 | tf_op jit(solution)/shard_map/all_to_all | solution.py:427
  37.8 8.6 %intra.1 = (f32[1,320,4096]{2,1,0:T(8,128)}, bf16[1,320,4096]{2,1,0:T(8,128)(2,1)}) custom-call(bf16[1,320,4096]{2,1,0:T(8,128)(2,1)} %q_ref.3, bf16[1,320,4096]{2,1,0:T(8,128)(2,1)} %k_ref.7, bf16[1,320,4096]{2,1,0:T(8,128)(2,1)} %v_ref.7, f32[4,320,8]{2,1,0:T(8,128)S(1)} %get-tuple-element.25.col_ref, f32[4,8,320]{2,1,0:T(8,128)S(1)} %get-tuple-element.26.row_ref), custom_call_target="tpu_custom_call" | custom-call | flops 1677721600 | bytes 23592960 | tf_op jit(solution)/shard_map/intra/pallas_call | solution.py:430
  46.4 6.5 %all-to-all-done.1 = bf16[16,256,128]{2,1,0:T(8,128)(2,1)S(1)} async-done(((bf16[16,256,128]{2,1,0:T(8,128)(2,1)}), bf16[16,256,128]{2,1,0:T(8,128)(2,1)S(1)}, u32[]{:S(2)}, u32[]{:S(2)}) %all-to-all-start.1) | async-done | bytes 1048608 | tf_op jit(solution)/shard_map/all_to_all | solution.py:427
  53.0 8.4 %norm.1 = (bf16[1,320,4096]{2,1,0:T(8,128)(2,1)}, bf16[1,320,4096]{2,1,0:T(8,128)(2,1)}, bf16[32,128,128]{2,1,0:T(8,128)(2,1)S(1)}) custom-call(f32[1,320,4096]{2,1,0:T(8,128)} %get-tuple-element.27.raw_ref, bf16[1,320,4096]{2,1,0:T(8,128)(2,1)} %get-tuple-element.28.scaled_ref, bf16[1,320,4096]{2,1,0:T(8,128)(2,1)} %g_ref.1, bf16[32,128,128]{2,1,0:T(8,128)(2,1)S(1)} %bitcast.7), custom_call_target="tpu_custom_call" | custom-call | tf_op jit(solution)/shard_map/norm/pallas_call | solution.py:442
  61.4 0.0 copy-start.1
  61.4 1.0 copy-done.1
  62.4 3.7 %all-to-all-start.2 = ((bf16[16,256,128]{2,1,0:T(8,128)(2,1)}), bf16[16,256,128]{2,1,0:T(8,128)(2,1)S(1)}, u32[]{:S(2)}, u32[]{:S(2)}) async-start(bf16[16,256,128]{2,1,0:T(8,128)(2,1)} %bitcast.10), calls=%async_computation.2 | async-start | bytes 2097152 | tf_op jit(solution)/shard_map/all_to_all | solution.py:453
  66.0 9.0 %grad_q.1 = (bf16[1,320,4096]{2,1,0:T(8,128)(2,1)}, bf16[32,320,128]{2,1,0:T(8,128)(2,1)}) custom-call(bf16[1,320,4096]{2,1,0:T(8,128)(2,1)} %get-tuple-element.32.grad_raw_ref, bf16[1,320,4096]{2,1,0:T(8,128)(2,1)} %k_ref.7, bf16[1,320,4096]{2,1,0:T(8,128)(2,1)} %v_ref.7, f32[4,320,8]{2,1,0:T(8,128)S(1)} %get-tuple-element.25.col_ref, ...), custom_call_target="tpu_custom_call" | custom-call | flops 1677721600 | bytes 15728640 | tf_op jit(solution)/shard_map/grad_q/pallas_call | solution.py:455
  75.0 6.9 %all-to-all-done.2.x_ref = bf16[16,256,128]{2,1,0:T(8,128)(2,1)S(1)} async-done(((bf16[16,256,128]{2,1,0:T(8,128)(2,1)}), bf16[16,256,128]{2,1,0:T(8,128)(2,1)S(1)}, u32[]{:S(2)}, u32[]{:S(2)}) %all-to-all-start.2) | async-done | bytes 1048608 | tf_op jit(solution)/shard_map/all_to_all | solution.py:453
  81.9 1.2 second_scan.1
  83.1 3.7 %all-to-all-start.3 = ((bf16[16,256,128]{2,1,0:T(8,128)(2,1)}), bf16[16,256,128]{2,1,0:T(8,128)(2,1)S(1)}, u32[]{:S(2)}, u32[]{:S(2)}) async-start(bf16[16,256,128]{2,1,0:T(8,128)(2,1)} %second_scan.1), calls=%async_computation.3 | async-start | bytes 2097152 | tf_op jit(solution)/shard_map/all_to_all | solution.py:476
  86.8 0.0 copy-start.3
  86.8 14.1 %grad_kv.1 = (bf16[1,320,4096]{2,1,0:T(8,128)(2,1)}, bf16[1,320,4096]{2,1,0:T(8,128)(2,1)}, bf16[1,320,4096]{2,1,0:T(8,128)(2,1)}, bf16[1,320,4096]{2,1,0:T(8,128)(2,1)}) custom-call(bf16[1,320,4096]{2,1,0:T(8,128)(2,1)} %get-tuple-element.32.grad_raw_ref, bf16[1,320,4096]{2,1,0:T(8,128)(2,1)} %q_ref.3, bf16[1,320,4096]{2,1,0:T(8,128)(2,1)} %k_ref.7, ...), custom_call_target="tpu_custom_call" | custom-call | flops 3355443200 | bytes 20971520 | tf_op jit(solution)/shard_map/grad_kv/pallas_call | solution.py:479
  100.9 1.6 all-to-all-done.3
  102.5 0.0 copy-done.3
  102.5 14.0 %kept.1 = (bf16[1,320,4096]{2,1,0:T(8,128)(2,1)}, bf16[1,320,4096]{2,1,0:T(8,128)(2,1)}, bf16[64,128,128]{2,1,0:T(8,128)(2,1)S(1)}, bf16[64,128,128]{2,1,0:T(8,128)(2,1)S(1)}) custom-call(s32[128]{0:T(128)S(1)} %copy-done.3, s32[1]{0:T(128)} %bitcast.2.core_ref, bf16[1,320,4096]{2,1,0:T(8,128)(2,1)} %get-tuple-element.34.scaled_k_ref, ...), custom_call_target="tpu_custom_call" | custom-call | tf_op jit(solution)/shard_map/kept/pallas_call | solution.py:493
  116.6 0.1 collective-permute-start
  116.7 4.1 %collective-permute-done = bf16[64,128,128]{2,1,0:T(8,128)(2,1)S(1)} collective-permute-done((bf16[64,128,128]{2,1,0:T(8,128)(2,1)S(1)}, bf16[64,128,128]{2,1,0:T(8,128)(2,1)S(1)}, u32[]{:S(2)}, u32[]{:S(2)}) %collective-permute-start) | collective-permute-done | bytes 2097184 | tf_op jit(solution)/shard_map/ppermute | solution.py:520
  120.8 0.8 add_convert_fusion
  121.6 39.7 %all_to_all.25 = bf16[64,128,128]{2,1,0:T(8,128)(2,1)S(1)} all-to-all(bf16[64,128,128]{2,1,0:T(8,128)(2,1)S(1)} %add_convert_fusion), channel_id=1, replica_groups=mesh['x'=4,'y'=4,'z'=4,'core'=2] {'x','y','z'}, dimensions={0} | all-to-all | bytes 4194304 | tf_op jit(solution)/shard_map/all_to_all | solution.py:522
  161.4 0.3 convert_reduce_fusion
  161.7 0.6 multiply_bitcast_fusion
Async XLA Ops:
  6.3 1.0 copy-start
  7.3 25.6 %all-to-all-start = ((bf16[16,272,128]{2,1,0:T(8,128)(2,1)}), bf16[16,272,128]{2,1,0:T(8,128)(2,1)S(1)}, u32[]{:S(2)}, u32[]{:S(2)}) async-start(bf16[16,272,128]{2,1,0:T(8,128)(2,1)} %copy-done), calls=%async_computation | async-start | bytes 2228224 | tf_op jit(solution)/shard_map/all_to_all | solution.py:403
  33.2 1.0 copy-start.2
  34.2 18.8 %all-to-all-start.1 = ((bf16[16,256,128]{2,1,0:T(8,128)(2,1)}), bf16[16,256,128]{2,1,0:T(8,128)(2,1)S(1)}, u32[]{:S(2)}, u32[]{:S(2)}) async-start(bf16[16,256,128]{2,1,0:T(8,128)(2,1)} %copy-done.2), calls=%async_computation.1 | async-start | bytes 2097152 | tf_op jit(solution)/shard_map/all_to_all | solution.py:427
  61.4 1.0 copy-start.1
  62.4 19.6 %all-to-all-start.2 = ((bf16[16,256,128]{2,1,0:T(8,128)(2,1)}), bf16[16,256,128]{2,1,0:T(8,128)(2,1)S(1)}, u32[]{:S(2)}, u32[]{:S(2)}) async-start(bf16[16,256,128]{2,1,0:T(8,128)(2,1)} %bitcast.10), calls=%async_computation.2 | async-start | bytes 2097152 | tf_op jit(solution)/shard_map/all_to_all | solution.py:453
  83.1 19.4 %all-to-all-start.3 = ((bf16[16,256,128]{2,1,0:T(8,128)(2,1)}), bf16[16,256,128]{2,1,0:T(8,128)(2,1)S(1)}, u32[]{:S(2)}, u32[]{:S(2)}) async-start(bf16[16,256,128]{2,1,0:T(8,128)(2,1)} %second_scan.1), calls=%async_computation.3 | async-start | bytes 2097152 | tf_op jit(solution)/shard_map/all_to_all | solution.py:476
  86.8 15.8 %copy-start.3 = (s32[128]{0:T(128)S(1)}, s32[128]{0:T(128)}, u32[]{:S(2)}) copy-start(s32[128]{0:T(128)} %kept_ref.1) | copy-start | bytes 1540
  116.6 4.2 %collective-permute-start = (bf16[64,128,128]{2,1,0:T(8,128)(2,1)S(1)}, bf16[64,128,128]{2,1,0:T(8,128)(2,1)S(1)}, u32[]{:S(2)}, u32[]{:S(2)}) collective-permute-start(bf16[64,128,128]{2,1,0:T(8,128)(2,1)S(1)} %get-tuple-element.44), channel_id=1, source_target_pairs={{0,1},{1,0},{2,3},{3,2},{4,5},{5,4},{6,7},{7,6},{8,9},{9,8},{10,11... | collective-permute-start | bytes 6291464 | tf_op jit(solution)/shard_map/ppermute | solution.py:520

commit v3 on v2

--- a/solution.py
+++ b/solution.py
@@ -39,49 +39,81 @@
     return [range(h, h + size) for h in range(0, GROUP, size)]
 
 
-def states_kernel(decay_ref, k_ref, v_ref, payload_ref, col_ref, row_ref):
-    length = k_ref.shape[1]
-    group = pl.program_id(0)
+def group_lanes(g):
+    return slice(g * GROUP * BLOCK, (g + 1) * GROUP * BLOCK)
+
+
+def start_loads(pairs, groups, sems, first=0):
+    loads = []
+    for g in range(groups):
+        at = group_lanes(g)
+        copies = [
+            pltpu.make_async_copy(source.at[0, :, at], buffer.at[:, at], sems.at[first + g * len(pairs) + n])
+            for n, (source, buffer) in enumerate(pairs)
+        ]
+        for copy in copies:
+            copy.start()
+        loads.append(copies)
+    return loads
+
+
+def states_kernel(
+    decay_hbm, k_hbm, v_hbm, payload_hbm, col_ref, row_ref, decay_ref, k_ref, v_ref, payload, sems
+):
+    length = k_ref.shape[0]
     groups = col_ref.shape[0]
     heads = groups * GROUP
-
-    @pl.when(group == 0)
-    def _():
-        decay = decay_ref[...]
-        high = decay.astype(BF16).astype(F32)
-        rest = decay - high
-        middle = rest.astype(BF16).astype(F32)
-        terms = jnp.concatenate([high, middle, rest - middle], axis=0).astype(BF16)
-        t = lax.broadcasted_iota(jnp.int32, (length, length), 0)
-        s = lax.broadcasted_iota(jnp.int32, (length, length), 1)
-        lower = jnp.where(s <= t, 1.0, 0.0).astype(BF16)
-        upper = jnp.where(t <= s, 1.0, 0.0).astype(BF16)
-        cols = dot_nt(lower, terms)
-        rows = dot_nn(terms, upper)
-        row = rows[:heads] + rows[heads : 2 * heads] + rows[2 * heads :]
-        for g in range(groups):
-            at = [slice(n * heads + g * GROUP, n * heads + (g + 1) * GROUP) for n in range(3)]
-            col_ref[g] = cols[:, at[0]] + cols[:, at[1]] + cols[:, at[2]]
-            row_ref[g] = row[g * GROUP : (g + 1) * GROUP]
-
-    col = col_ref[group]
-    total = col[length - 1 : length, :]
-    tail = jnp.exp(total - col)
+    owners = GROUP // 2
+    load_decay = pltpu.make_async_copy(decay_hbm, decay_ref, sems.at[3 * groups])
+    load_decay.start()
+    loads = start_loads([(k_hbm, k_ref), (v_hbm, v_ref)], groups, sems)
+    load_decay.wait()
+
+    decay = decay_ref[...]
+    high = decay.astype(BF16).astype(F32)
+    rest = decay - high
+    middle = rest.astype(BF16).astype(F32)
+    terms = jnp.concatenate([high, middle, rest - middle], axis=0).astype(BF16)
+    t = lax.broadcasted_iota(jnp.int32, (length, length), 0)
+    s = lax.broadcasted_iota(jnp.int32, (length, length), 1)
+    lower = jnp.where(s <= t, 1.0, 0.0).astype(BF16)
+    upper = jnp.where(t <= s, 1.0, 0.0).astype(BF16)
+    cols = dot_nt(lower, terms)
+    rows = dot_nn(terms, upper)
+    row = rows[:heads] + rows[heads : 2 * heads] + rows[2 * heads :]
+    cols = cols[:, :heads] + cols[:, heads : 2 * heads] + cols[:, 2 * heads :]
+    total = cols[length - 1 : length, :]
+    tails = jnp.exp(total - cols)
     whole = jnp.exp(total)
     index = lax.broadcasted_iota(jnp.int32, (AUX, BLOCK), 0)
-    for hs in batches(4):
-        scaled = [v_ref[0, :, head_slice(h)].astype(F32) * tail[:, h : h + 1] for h in hs]
-        states = [dot_tn(k_ref[0, :, head_slice(h)], x.astype(BF16)) for h, x in zip(hs, scaled)]
-        for h, state in zip(hs, states):
-            payload_ref[h // 2, head_slice(h % 2), :] = state.astype(BF16)
-    for p in range(GROUP // 2):
+    for g in range(groups):
+        col_ref[g] = cols[:, g * GROUP : (g + 1) * GROUP]
+        row_ref[g] = row[g * GROUP : (g + 1) * GROUP]
+    for p in range(heads // 2):
         aux = jnp.zeros((AUX, BLOCK), F32)
         for i in range(2):
             value = jnp.broadcast_to(whole[:, 2 * p + i : 2 * p + i + 1], (AUX, BLOCK))
             first = value.astype(BF16).astype(F32)
             aux = jnp.where(index == 2 * i, first, aux)
             aux = jnp.where(index == 2 * i + 1, value - first, aux)
-        payload_ref[p, 2 * BLOCK :, :] = aux.astype(BF16)
+        payload[p, 2 * BLOCK :, :] = aux.astype(BF16)
+
+    stores = []
+    for g in range(groups):
+        for copy in loads[g]:
+            copy.wait()
+        for batch in batches(4):
+            hs = [g * GROUP + h for h in batch]
+            scaled = [v_ref[:, head_slice(h)].astype(F32) * tails[:, h : h + 1] for h in hs]
+            states = [dot_tn(k_ref[:, head_slice(h)], x.astype(BF16)) for h, x in zip(hs, scaled)]
+            for h, state in zip(hs, states):
+                payload[h // 2, head_slice(h % 2), :] = state.astype(BF16)
+        at = pl.ds(g * owners, owners)
+        store = pltpu.make_async_copy(payload.at[at], payload_hbm.at[at], sems.at[2 * groups + g])
+        store.start()
+        stores.append(store)
+    for store in stores:
+        store.wait()
 
 
 def first_scan_kernel(x_ref, after_ref, out_ref, whole_ref):
@@ -143,28 +175,62 @@
 
 
 def norm_kernel(
-    raw_ref, scaled_ref, g_ref, carried_ref, attended_ref, grad_raw_ref, grad_ref
+    scaled_hbm,
+    raw_hbm,
+    g_hbm,
+    carried_ref,
+    attended_hbm,
+    grad_raw_hbm,
+    grad_hbm,
+    scaled_ref,
+    raw_ref,
+    g_ref,
+    attended_ref,
+    grad_raw_ref,
+    grad_ref,
+    sems,
 ):
-    for hs in batches(8):
+    groups = carried_ref.shape[0] // GROUP
+    pairs = [(scaled_hbm, scaled_ref), (raw_hbm, raw_ref), (g_hbm, g_ref)]
+    loads = start_loads(pairs, groups, sems)
+    stores = []
+    for group in range(groups):
+        for copy in loads[group]:
+            copy.wait()
+        hs = range(group * GROUP, (group + 1) * GROUP)
         sls = [head_slice(h) for h in hs]
-        raws = [dot_nn(scaled_ref[0, :, sl], carried_ref[h]) for h, sl in zip(hs, sls)]
-        raws = [raw + raw_ref[0, :, sl] for raw, sl in zip(raws, sls)]
+        raws = [dot_nn(scaled_ref[:, sl], carried_ref[h]) for h, sl in zip(hs, sls)]
+        raws = [raw + raw_ref[:, sl] for raw, sl in zip(raws, sls)]
         squares = [jnp.mean(raw * raw, axis=1, keepdims=True) for raw in raws]
         shareds = [
-            jnp.mean(g_ref[0, :, sl].astype(F32) * raw, axis=1, keepdims=True)
+            jnp.mean(g_ref[:, sl].astype(F32) * raw, axis=1, keepdims=True)
             for raw, sl in zip(raws, sls)
         ]
         inverses = [lax.rsqrt(square + 1e-6) for square in squares]
         grads = []
         for raw, inverse, shared, sl in zip(raws, inverses, shareds, sls):
             normed = raw * inverse
-            attended_ref[0, :, sl] = normed.astype(BF16)
-            upstream = g_ref[0, :, sl].astype(F32)
+            attended_ref[:, sl] = normed.astype(BF16)
+            upstream = g_ref[:, sl].astype(F32)
             grad_raw = (inverse * (upstream - normed * (shared * inverse))).astype(BF16)
-            grad_raw_ref[0, :, sl] = grad_raw
+            grad_raw_ref[:, sl] = grad_raw
             grads.append(grad_raw)
         for h, sl, grad_raw in zip(hs, sls, grads):
-            grad_ref[h] = dot_tn(scaled_ref[0, :, sl], grad_raw).astype(BF16)
+            grad_ref[h] = dot_tn(scaled_ref[:, sl], grad_raw).astype(BF16)
+        at = group_lanes(group)
+        heads = pl.ds(group * GROUP, GROUP)
+        for n, (source, target) in enumerate(
+            (
+                (grad_ref.at[heads], grad_hbm.at[heads]),
+                (grad_raw_ref.at[:, at], grad_raw_hbm.at[0, :, at]),
+                (attended_ref.at[:, at], attended_hbm.at[0, :, at]),
+            )
+        ):
+            store = pltpu.make_async_copy(source, target, sems.at[3 * groups + 3 * group + n])
+            store.start()
+            stores.append(store)
+    for store in stores:
+        store.wait()
 
 
 def grad_q_kernel(
@@ -252,68 +318,89 @@
             scaled_v_ref[0, :, sl] = (v_ref[0, :, sl].astype(F32) * factor).astype(BF16)
 
 
-def kept_kernel(
-    heads,
+def kept_products(kept_ref, turned, stack, out_ref, parity):
+    per_row = stack.shape[0]
+
+    def body(i, carry):
+        number = kept_ref[2 * i + parity]
+        left = turned[number // per_row]
+        right = stack[lax.rem(number, per_row)]
+        out_ref[i] = dot_nn(left, right).astype(BF16)
+        return carry
+
+    lax.fori_loop(0, out_ref.shape[0], body, 0, unroll=KEPT_UNROLL)
+
+
+def theirs_kernel(
     kept_ref,
     core_ref,
+    scaled_k_hbm,
+    scaled_v_hbm,
+    intra_k_hbm,
+    intra_v_hbm,
+    later_ref,
+    by_head_hbm,
+    turned_hbm,
+    grad_k_hbm,
+    grad_v_hbm,
+    theirs_ref,
+    stack,
+    turned,
     scaled_k_ref,
     scaled_v_ref,
     intra_k_ref,
     intra_v_ref,
-    later_ref,
-    by_head_ref,
-    turned_ref,
     grad_k_ref,
     grad_v_ref,
-    theirs_ref,
-    mine_ref,
-    stack,
-    turned,
-    stack_sem,
-    turned_sem,
+    sems,
 ):
-    group = pl.program_id(0)
-    copies = (
-        pltpu.make_async_copy(by_head_ref, stack.at[pl.ds(0, heads)], stack_sem),
-        pltpu.make_async_copy(turned_ref, turned, turned_sem),
+    heads = later_ref.shape[0]
+    groups = heads // GROUP
+    pairs = [
+        (scaled_v_hbm, scaled_v_ref),
+        (scaled_k_hbm, scaled_k_ref),
+        (intra_k_hbm, intra_k_ref),
+        (intra_v_hbm, intra_v_ref),
+    ]
+    loads = start_loads(pairs, groups, sems)
+    others = (
+        pltpu.make_async_copy(by_head_hbm, stack.at[pl.ds(0, heads)], sems.at[6 * groups]),
+        pltpu.make_async_copy(turned_hbm, turned, sems.at[6 * groups + 1]),
     )
-
-    @pl.when(group == 0)
-    def _():
-        for copy in copies:
-            copy.start()
-
-    for hs in batches(4):
-        sls = [head_slice(h) for h in hs]
-        grads_k = [dot_nt(scaled_v_ref[0, :, sl], later_ref[h]) for h, sl in zip(hs, sls)]
-        grads_v = [dot_nn(scaled_k_ref[0, :, sl], later_ref[h]) for h, sl in zip(hs, sls)]
-        for h, sl, grad_k, grad_v in zip(hs, sls, grads_k, grads_v):
-            grad_k = (intra_k_ref[0, :, sl].astype(F32) + grad_k).astype(BF16)
-            grad_v = (intra_v_ref[0, :, sl].astype(F32) + grad_v).astype(BF16)
-            grad_k_ref[0, :, sl] = grad_k
-            grad_v_ref[0, :, sl] = grad_v
-            stack[heads + group * GROUP + h] = grad_k
-            stack[2 * heads + group * GROUP + h] = grad_v
-
-    @pl.when(group == pl.num_programs(0) - 1)
-    def _():
-        for copy in copies:
+    for copy in others:
+        copy.start()
+    stores = []
+    for group in range(groups):
+        for copy in loads[group]:
             copy.wait()
-        core = core_ref[0]
-        per_row = 3 * heads
-
-        def run(out_ref, parity):
-            def body(i, carry):
-                number = kept_ref[2 * i + parity]
-                left = turned[number // per_row]
-                right = stack[lax.rem(number, per_row)]
-                out_ref[i] = dot_nn(left, right).astype(BF16)
-                return carry
-
-            lax.fori_loop(0, out_ref.shape[0], body, 0, unroll=KEPT_UNROLL)
-
-        run(theirs_ref, 1 - core)
-        run(mine_ref, core)
+        for batch in batches(4):
+            hs = [group * GROUP + h for h in batch]
+            sls = [head_slice(h) for h in hs]
+            grads_k = [dot_nt(scaled_v_ref[:, sl], later_ref[h]) for h, sl in zip(hs, sls)]
+            grads_v = [dot_nn(scaled_k_ref[:, sl], later_ref[h]) for h, sl in zip(hs, sls)]
+            for h, sl, grad_k, grad_v in zip(hs, sls, grads_k, grads_v):
+                grad_k = (intra_k_ref[:, sl].astype(F32) + grad_k).astype(BF16)
+                grad_v = (intra_v_ref[:, sl].astype(F32) + grad_v).astype(BF16)
+                grad_k_ref[:, sl] = grad_k
+                grad_v_ref[:, sl] = grad_v
+                stack[heads + h] = grad_k
+                stack[2 * heads + h] = grad_v
+        at = group_lanes(group)
+        for n, (source, target) in enumerate(((grad_k_ref, grad_k_hbm), (grad_v_ref, grad_v_hbm))):
+            store = pltpu.make_async_copy(
+                source.at[:, at], target.at[0, :, at], sems.at[4 * groups + 2 * group + n]
+            )
+            store.start()
+            stores.append(store)
+    for copy in others:
+        copy.wait()
+    kept_products(kept_ref, turned, stack, theirs_ref, 1 - core_ref[0])
+    for store in stores:
+        store.wait()
+
+
+def mine_kernel(kept_ref, core_ref, stack, turned, mine_ref):
+    kept_products(kept_ref, turned, stack, mine_ref, core_ref[0])
 
 
 def in_hbm(x):
@@ -381,22 +468,26 @@
     grad_attended, layer_input = in_hbm(grad_attended), in_hbm(layer_input)
     decay = in_hbm(log_decay[0])
 
+    tall = (length, width)
     payload, col, row = call(
         "states",
         states_kernel,
-        (groups,),
-        [at_start(heads, length), tokens, tokens],
+        (),
+        [anywhere, anywhere, anywhere],
+        [anywhere, whole, whole],
         [
-            pl.BlockSpec((pair, rows + AUX, BLOCK), lambda g: (g, 0, 0)),
-            at_start(groups, length, GROUP),
-            at_start(groups, GROUP, length),
-        ],
-        [
-            vmem((blocks, rows + AUX, BLOCK), BF16),
+            hbm((blocks, rows + AUX, BLOCK), BF16),
             vmem((groups, length, GROUP), F32),
             vmem((groups, GROUP, length), F32),
         ],
-        16,
+        24,
+        scratch=[
+            pltpu.VMEM((heads, length), F32),
+            pltpu.VMEM(tall, BF16),
+            pltpu.VMEM(tall, BF16),
+            pltpu.VMEM((blocks, rows + AUX, BLOCK), BF16),
+            pltpu.SemaphoreType.DMA((3 * groups + 1,)),
+        ],
     )(decay, key_vectors, value_vectors)
     col, row = in_vmem(col), in_vmem(row)
 
@@ -421,7 +512,7 @@
         (),
         [whole, anywhere],
         [whole, whole],
-        [vmem((blocks, rows, BLOCK), BF16), vmem((blocks, 8, BLOCK), F32)],
+        [hbm((blocks, rows, BLOCK), BF16), vmem((blocks, 8, BLOCK), F32)],
         8,
     )(in_vmem(received), turned)
     carried = lax.all_to_all(scanned, seq, 0, 0, tiled=True)
@@ -442,12 +533,21 @@
     attended, grad_raw, block_grad = call(
         "norm",
         norm_kernel,
-        (groups,),
-        [tokens, tokens, tokens, square],
-        [tokens, tokens, square],
-        [hbm(flat, BF16), hbm(flat, BF16), vmem((heads, BLOCK, BLOCK), BF16)],
+        (),
+        [anywhere, anywhere, anywhere, whole],
+        [anywhere, anywhere, anywhere],
+        [hbm(flat, BF16), hbm(flat, BF16), hbm((heads, BLOCK, BLOCK), BF16)],
         32,
-    )(intra, scaled_q, grad_attended, carried)
+        scratch=[
+            pltpu.VMEM(tall, BF16),
+            pltpu.VMEM(tall, F32),
+            pltpu.VMEM(tall, BF16),
+            pltpu.VMEM(tall, BF16),
+            pltpu.VMEM(tall, BF16),
+            pltpu.VMEM((heads, BLOCK, BLOCK), BF16),
+            pltpu.SemaphoreType.DMA((6 * groups,)),
+        ],
+    )(scaled_q, intra, grad_attended, carried)
     grad_raw = in_hbm(grad_raw)
 
     sent = lax.all_to_all(block_grad.reshape(blocks, rows, BLOCK), seq, 0, 0, tiled=True)
@@ -470,7 +570,7 @@
         (),
         [whole, whole, anywhere],
         whole,
-        vmem((blocks, rows, BLOCK), BF16),
+        hbm((blocks, rows, BLOCK), BF16),
         8,
     )(in_vmem(sent), in_vmem(whole_decay), grad_q_by_head)
     later = lax.all_to_all(scanned, seq, 0, 0, tiled=True)
@@ -490,20 +590,30 @@
 
     core = lax.axis_index("core").astype(jnp.int32).reshape(1)
     half = (kept // 2, BLOCK, BLOCK)
-    grad_k, grad_v, theirs, mine = call(
-        "kept",
-        functools.partial(kept_kernel, heads),
-        (groups,),
-        [tokens, tokens, tokens, tokens, square, anywhere, anywhere],
-        [tokens, tokens, at_start(*half), at_start(*half)],
-        [hbm(flat, BF16), hbm(flat, BF16), vmem(half, BF16), vmem(half, BF16)],
-        44,
+    stack_shape = (3 * heads, length, BLOCK)
+    grad_k, grad_v, theirs, stack, turned = call(
+        "theirs",
+        theirs_kernel,
+        (),
+        [anywhere, anywhere, anywhere, anywhere, whole, anywhere, anywhere],
+        [anywhere, anywhere, whole, whole, whole],
+        [
+            hbm(flat, BF16),
+            hbm(flat, BF16),
+            vmem(half, BF16),
+            vmem(stack_shape, BF16),
+            vmem(turned.shape, BF16),
+        ],
+        40,
         prefetch=2,
         scratch=[
-            pltpu.VMEM((3 * heads, length, BLOCK), BF16),
-            pltpu.VMEM(turned.shape, BF16),
-            pltpu.SemaphoreType.DMA,
-            pltpu.SemaphoreType.DMA,
+            pltpu.VMEM(tall, BF16),
+            pltpu.VMEM(tall, BF16),
+            pltpu.VMEM(tall, BF16),
+            pltpu.VMEM(tall, BF16),
+            pltpu.VMEM(tall, BF16),
+            pltpu.VMEM(tall, BF16),
+            pltpu.SemaphoreType.DMA((6 * groups + 2,)),
         ],
     )(
         kept_blocks,
@@ -516,6 +626,17 @@
         grad_q_by_head,
         turned,
     )
+    mine = call(
+        "mine",
+        mine_kernel,
+        (),
+        [whole, whole],
+        whole,
+        vmem(half, BF16),
+        20,
+        (2 * kept * length * BLOCK * BLOCK, kept * BLOCK * BLOCK * 2),
+        prefetch=2,
+    )(kept_blocks, core, in_vmem(stack), in_vmem(turned))
 
     other = lax.ppermute(theirs, "core", [(0, 1), (1, 0)])
     chip = (mine.astype(F32) + other.astype(F32)).astype(BF16)

time: 163 us -> 159 us (0.975)
  waiting for transfers between devices: 31.4 us -> 28.3 us
  local copies, waits for them, and re-layouts: 2.93 us -> 0.01 us
    unnamed x8 -> x2, local copies, waits for them, and re-layouts: 2.93 us -> 0.01 us
    ppermute x1, waiting for transfers between devices: 4.15 us -> 1.33 us  [per_device(): other = lax.ppermute(theirs, 'core', [(0, 1), (1, 0)])]
    pallas_call x3 -> x4, Pallas kernels: 28.1 us -> 28.1 us  [the longest x1 11.4 us: per_device(): call('theirs', theirs_kernel, (), [anywhere, anywhere, anywhere, anywhere...]
  transfers between devices with their start and end apart: 5 -> 5, of which waited for: 5 -> 5; matrix products, arithmetic and copies ran while one was open for 0% -> 0% of each run, Pallas kernels for 23% -> 26%
where the time goes in v3:
time: 159 us; the launch traced here: 158 us
  Pallas kernels  68.7 us (43%)
  blocking collectives  39.7 us (25%)
  waiting for transfers between devices  28.3 us (18%)
  starting transfers between devices  18.4 us (12%)
  other arithmetic  2.04 us (1%)
    all_to_all x1, blocking collectives, per_device(): parts = lax.all_to_all(chip, ('x', 'y', 'z'), 0, 0, tiled=True)  39.7 us
    pallas_call x1, Pallas kernels, per_device(): call('grad_kv', grad_kv_kernel, (groups,), [tokens, tokens, tokens, token...  14.1 us
    all_to_all x1, waiting for transfers between devices, per_device(): received = lax.all_to_all(payload, seq, 0, 0, tiled=True)  12.1 us
    pallas_call x1, Pallas kernels, per_device(): call('theirs', theirs_kernel, (), [anywhere, anywhere, anywhere, anywhere...  11.4 us
    pallas_call x1, Pallas kernels, per_device(): call('grad_q', grad_q_kernel, (groups,), [tokens, tokens, tokens, col_spe...  8.95 us
    pallas_call x1, Pallas kernels, per_device(): call('intra', intra_kernel, (groups,), [tokens, tokens, tokens, col_spec,...  8.72 us
    pallas_call x1, Pallas kernels, per_device(): call('norm', norm_kernel, (), [anywhere, anywhere, anywhere, whole], [any...  8.58 us
    all_to_all x1, starting transfers between devices, per_device(): received = lax.all_to_all(payload, seq, 0, 0, tiled=True)  7.13 us
  transfers between devices with their start and end apart: 5, of which 5 were waited for; matrix products, arithmetic and copies ran while one was open for 0% of the time, Pallas kernels for 26%

profile of v3, /device:TPU:0, one launch (start us, length us, event | category | flops | bytes accessed | tf_op | source)
XLA Modules:
  0.0 157.8 jit_solution(17971662259857601939)
XLA Ops:
  0.6 5.3 %states.1 = (bf16[16,272,128]{2,1,0:T(8,128)(2,1)}, f32[4,320,8]{2,1,0:T(8,128)S(1)}, f32[4,8,320]{2,1,0:T(8,128)S(1)}) custom-call(f32[32,320]{1,0:T(8,128)} %bitcast.11, bf16[1,320,4096]{2,1,0:T(8,128)(2,1)} %k_ref.5, bf16[1,320,4096]{2,1,0:T(8,128)(2,1)} %v_ref.5), custom_call_target="tpu_custom_call" | custom-call | tf_op jit(solution)/shard_map/states/pallas_call | solution.py:472
  6.0 7.1 %all-to-all-start = ((bf16[16,272,128]{2,1,0:T(8,128)(2,1)}), bf16[16,272,128]{2,1,0:T(8,128)(2,1)S(1)}, u32[]{:S(2)}, u32[]{:S(2)}) async-start(bf16[16,272,128]{2,1,0:T(8,128)(2,1)} %get-tuple-element.30), calls=%async_computation | async-start | bytes 2228224 | tf_op jit(solution)/shard_map/all_to_all | solution.py:494
  13.1 6.4 %turn.1.after_ref.turned_hbm = bf16[48,128,320]{2,1,0:T(8,128)(2,1)} custom-call(bf16[1,320,6144]{2,1,0:T(8,128)(2,1)} %x_ref.1), custom_call_target="tpu_custom_call" | custom-call | flops 838860800 | bytes 7864320 | tf_op jit(solution)/shard_map/turn/pallas_call | solution.py:497
  19.5 12.1 %all-to-all-done.x_ref = bf16[16,272,128]{2,1,0:T(8,128)(2,1)S(1)} async-done(((bf16[16,272,128]{2,1,0:T(8,128)(2,1)}), bf16[16,272,128]{2,1,0:T(8,128)(2,1)S(1)}, u32[]{:S(2)}, u32[]{:S(2)}) %all-to-all-start) | async-done | bytes 1114144 | tf_op jit(solution)/shard_map/all_to_all | solution.py:494
  31.6 1.2 first_scan.1
  32.8 3.7 %all-to-all-start.1 = ((bf16[16,256,128]{2,1,0:T(8,128)(2,1)}), bf16[16,256,128]{2,1,0:T(8,128)(2,1)S(1)}, u32[]{:S(2)}, u32[]{:S(2)}) async-start(bf16[16,256,128]{2,1,0:T(8,128)(2,1)} %get-tuple-element.31), calls=%async_computation.1 | async-start | bytes 2097152 | tf_op jit(solution)/shard_map/all_to_all | solution.py:518
  36.5 8.7 %intra.1 = (f32[1,320,4096]{2,1,0:T(8,128)}, bf16[1,320,4096]{2,1,0:T(8,128)(2,1)}) custom-call(bf16[1,320,4096]{2,1,0:T(8,128)(2,1)} %q_ref.3, bf16[1,320,4096]{2,1,0:T(8,128)(2,1)} %k_ref.5, bf16[1,320,4096]{2,1,0:T(8,128)(2,1)} %v_ref.5, f32[4,320,8]{2,1,0:T(8,128)S(1)} %get-tuple-element.26.col_ref, f32[4,8,320]{2,1,0:T(8,128)S(1)} %get-tuple-element.27.row_ref), custom_call_target="tpu_custom_call" | custom-call | flops 1677721600 | bytes 23592960 | tf_op jit(solution)/shard_map/intra/pallas_call | solution.py:521
  45.2 6.5 %all-to-all-done.1 = bf16[16,256,128]{2,1,0:T(8,128)(2,1)S(1)} async-done(((bf16[16,256,128]{2,1,0:T(8,128)(2,1)}), bf16[16,256,128]{2,1,0:T(8,128)(2,1)S(1)}, u32[]{:S(2)}, u32[]{:S(2)}) %all-to-all-start.1) | async-done | bytes 1048608 | tf_op jit(solution)/shard_map/all_to_all | solution.py:518
  51.7 8.6 %norm.1 = (bf16[1,320,4096]{2,1,0:T(8,128)(2,1)}, bf16[1,320,4096]{2,1,0:T(8,128)(2,1)}, bf16[32,128,128]{2,1,0:T(8,128)(2,1)}) custom-call(bf16[1,320,4096]{2,1,0:T(8,128)(2,1)} %get-tuple-element.28.scaled_hbm, f32[1,320,4096]{2,1,0:T(8,128)} %get-tuple-element.29.raw_hbm, bf16[1,320,4096]{2,1,0:T(8,128)(2,1)} %g_hbm.1, bf16[32,128,128]{2,1,0:T(8,128)(2,1)S(1)} %bitcast.7), custom_call_target="tpu_custom_call" | custom-call | tf_op jit(solution)/shard_map/norm/pallas_call | solution.py:533
  60.3 3.8 %all-to-all-start.2 = ((bf16[16,256,128]{2,1,0:T(8,128)(2,1)}), bf16[16,256,128]{2,1,0:T(8,128)(2,1)S(1)}, u32[]{:S(2)}, u32[]{:S(2)}) async-start(bf16[16,256,128]{2,1,0:T(8,128)(2,1)} %bitcast.10), calls=%async_computation.2 | async-start | bytes 2097152 | tf_op jit(solution)/shard_map/all_to_all | solution.py:553
  64.1 8.9 %grad_q.1 = (bf16[1,320,4096]{2,1,0:T(8,128)(2,1)}, bf16[32,320,128]{2,1,0:T(8,128)(2,1)}) custom-call(bf16[1,320,4096]{2,1,0:T(8,128)(2,1)} %get-tuple-element.33.grad_raw_ref, bf16[1,320,4096]{2,1,0:T(8,128)(2,1)} %k_ref.5, bf16[1,320,4096]{2,1,0:T(8,128)(2,1)} %v_ref.5, f32[4,320,8]{2,1,0:T(8,128)S(1)} %get-tuple-element.26.col_ref, ...), custom_call_target="tpu_custom_call" | custom-call | flops 1677721600 | bytes 15728640 | tf_op jit(solution)/shard_map/grad_q/pallas_call | solution.py:555
  73.1 6.8 %all-to-all-done.2.x_ref = bf16[16,256,128]{2,1,0:T(8,128)(2,1)S(1)} async-done(((bf16[16,256,128]{2,1,0:T(8,128)(2,1)}), bf16[16,256,128]{2,1,0:T(8,128)(2,1)S(1)}, u32[]{:S(2)}, u32[]{:S(2)}) %all-to-all-start.2) | async-done | bytes 1048608 | tf_op jit(solution)/shard_map/all_to_all | solution.py:553
  79.8 1.2 second_scan.1
  81.0 3.7 %all-to-all-start.3 = ((bf16[16,256,128]{2,1,0:T(8,128)(2,1)}), bf16[16,256,128]{2,1,0:T(8,128)(2,1)S(1)}, u32[]{:S(2)}, u32[]{:S(2)}) async-start(bf16[16,256,128]{2,1,0:T(8,128)(2,1)} %second_scan.1), calls=%async_computation.3 | async-start | bytes 2097152 | tf_op jit(solution)/shard_map/all_to_all | solution.py:576
  84.7 14.1 %grad_kv.1 = (bf16[1,320,4096]{2,1,0:T(8,128)(2,1)}, bf16[1,320,4096]{2,1,0:T(8,128)(2,1)}, bf16[1,320,4096]{2,1,0:T(8,128)(2,1)}, bf16[1,320,4096]{2,1,0:T(8,128)(2,1)}) custom-call(bf16[1,320,4096]{2,1,0:T(8,128)(2,1)} %get-tuple-element.33.grad_raw_ref, bf16[1,320,4096]{2,1,0:T(8,128)(2,1)} %q_ref.3, bf16[1,320,4096]{2,1,0:T(8,128)(2,1)} %k_ref.5, ...), custom_call_target="tpu_custom_call" | custom-call | flops 3355443200 | bytes 20971520 | tf_op jit(solution)/shard_map/grad_kv/pallas_call | solution.py:579
  98.8 1.6 %all-to-all-done.3 = bf16[16,256,128]{2,1,0:T(8,128)(2,1)S(1)} async-done(((bf16[16,256,128]{2,1,0:T(8,128)(2,1)}), bf16[16,256,128]{2,1,0:T(8,128)(2,1)S(1)}, u32[]{:S(2)}, u32[]{:S(2)}) %all-to-all-start.3) | async-done | bytes 1048608 | tf_op jit(solution)/shard_map/all_to_all | solution.py:576
  100.4 0.0 copy-start
  100.4 11.4 %theirs.1 = (bf16[1,320,4096]{2,1,0:T(8,128)(2,1)}, bf16[1,320,4096]{2,1,0:T(8,128)(2,1)}, bf16[64,128,128]{2,1,0:T(8,128)(2,1)S(1)}, bf16[96,320,128]{2,1,0:T(8,128)(2,1)S(1)}, bf16[48,128,320]{2,1,0:T(8,128)(2,1)S(1)}) custom-call(s32[128]{0:T(128)} %kept_ref.3, s32[1]{0:T(128)} %bitcast.2.core_ref, bf16[1,320,4096]{2,1,0:T(8,128)(2,1)} %get-tuple-element.35.scaled_k_hbm, ...), custom_call_target="tpu_custom_call" | custom-call | tf_op jit(solution)/shard_map/theirs/pallas_call | solution.py:594
  111.8 0.1 collective-permute-start
  111.9 0.0 copy-done
  111.9 2.8 %mine.1 = bf16[64,128,128]{2,1,0:T(8,128)(2,1)S(1)} custom-call(s32[128]{0:T(128)S(1)} %copy-done, s32[1]{0:T(128)} %bitcast.2.core_ref, bf16[96,320,128]{2,1,0:T(8,128)(2,1)S(1)} %get-tuple-element.44.stack, bf16[48,128,320]{2,1,0:T(8,128)(2,1)S(1)} %get-tuple-element.45.turned), custom_call_target="tpu_custom_call" | custom-call | flops 1342177280 | bytes 4194304 | tf_op jit(solution)/shard_map/mine/pallas_call | solution.py:629
  114.7 1.3 collective-permute-done
  116.1 1.1 add_convert_fusion
  117.2 39.7 %all_to_all.25 = bf16[64,128,128]{2,1,0:T(8,128)(2,1)S(1)} all-to-all(bf16[64,128,128]{2,1,0:T(8,128)(2,1)S(1)} %add_convert_fusion), channel_id=1, replica_groups=mesh['x'=4,'y'=4,'z'=4,'core'=2] {'x','y','z'}, dimensions={0} | all-to-all | bytes 4194304 | tf_op jit(solution)/shard_map/all_to_all | solution.py:643
  156.9 0.3 convert_reduce_fusion
  157.2 0.6 multiply_bitcast_fusion
Async XLA Ops:
  6.0 25.6 %all-to-all-start = ((bf16[16,272,128]{2,1,0:T(8,128)(2,1)}), bf16[16,272,128]{2,1,0:T(8,128)(2,1)S(1)}, u32[]{:S(2)}, u32[]{:S(2)}) async-start(bf16[16,272,128]{2,1,0:T(8,128)(2,1)} %get-tuple-element.30), calls=%async_computation | async-start | bytes 2228224 | tf_op jit(solution)/shard_map/all_to_all | solution.py:494
  32.8 18.8 %all-to-all-start.1 = ((bf16[16,256,128]{2,1,0:T(8,128)(2,1)}), bf16[16,256,128]{2,1,0:T(8,128)(2,1)S(1)}, u32[]{:S(2)}, u32[]{:S(2)}) async-start(bf16[16,256,128]{2,1,0:T(8,128)(2,1)} %get-tuple-element.31), calls=%async_computation.1 | async-start | bytes 2097152 | tf_op jit(solution)/shard_map/all_to_all | solution.py:518
  60.3 19.6 %all-to-all-start.2 = ((bf16[16,256,128]{2,1,0:T(8,128)(2,1)}), bf16[16,256,128]{2,1,0:T(8,128)(2,1)S(1)}, u32[]{:S(2)}, u32[]{:S(2)}) async-start(bf16[16,256,128]{2,1,0:T(8,128)(2,1)} %bitcast.10), calls=%async_computation.2 | async-start | bytes 2097152 | tf_op jit(solution)/shard_map/all_to_all | solution.py:553
  81.0 19.4 %all-to-all-start.3 = ((bf16[16,256,128]{2,1,0:T(8,128)(2,1)}), bf16[16,256,128]{2,1,0:T(8,128)(2,1)S(1)}, u32[]{:S(2)}, u32[]{:S(2)}) async-start(bf16[16,256,128]{2,1,0:T(8,128)(2,1)} %second_scan.1), calls=%async_computation.3 | async-start | bytes 2097152 | tf_op jit(solution)/shard_map/all_to_all | solution.py:576
  100.4 11.5 %copy-start = (s32[128]{0:T(128)S(1)}, s32[128]{0:T(128)}, u32[]{:S(2)}) copy-start(s32[128]{0:T(128)} %kept_ref.3) | copy-start | bytes 1540
  111.8 4.2 %collective-permute-start = (bf16[64,128,128]{2,1,0:T(8,128)(2,1)S(1)}, bf16[64,128,128]{2,1,0:T(8,128)(2,1)S(1)}, u32[]{:S(2)}, u32[]{:S(2)}) collective-permute-start(bf16[64,128,128]{2,1,0:T(8,128)(2,1)S(1)} %get-tuple-element.46), channel_id=1, source_target_pairs={{0,1},{1,0},{2,3},{3,2},{4,5},{5,4},{6,7},{7,6},{8,9},{9,8},{10,11... | collective-permute-start | bytes 6291464 | tf_op jit(solution)/shard_map/ppermute | solution.py:641
